TPU v7x, 256 devices: a whole 4x4x8 slice. The times are simulated.
256 devices in a mesh: fsdp: 32 (over x, z), rep: 8 (over y, core).
Axes of the slice: x: 4, y: 4, z: 8, core: 2. Of those that a mesh axis runs over, the one named last changes fastest.
Arguments:
- hidden: bfloat16 [4096, 16384], P('fsdp', 'rep'), may hold values from -6 to 6
- weight: bfloat16 [16384, 4096], P('fsdp', 'rep'), may hold values from -0.046875 to 0.046875
- gradient: bfloat16 [16384, 4096], P('fsdp', 'rep')
- stats_left: float32 [16384, 4096], P('fsdp', 'rep'), as said below
- stats_right: float32 [16384, 4096], P('fsdp', 'rep'), as said below
- root_left: float32 [16384, 4096], P('fsdp', 'rep'), as said below
- root_right: float32 [16384, 4096], P('fsdp', 'rep'), as said below
- due_rows: int32 [16, 8], replicated, may hold values from 0 to 31, as said below
Outputs:
- left_stats: float32 [16384, 4096], P('fsdp', 'rep')
- right_stats: float32 [16384, 4096], P('fsdp', 'rep')
- update: bfloat16 [16384, 4096], P('fsdp', 'rep')
- projected: bfloat16 [4096, 4096], P('fsdp', 'rep')
Inputs may be any that keep to these rules, and one draw needn't show every extreme that they name: `due_rows`: entry [i, j] is i or i + 16: of the blocks in rows i and i + 16 of block column j exactly that one is due. `stats_left`: each block is symmetric with a positive diagonal that exceeds the sum of magnitudes of its row's other entries. `stats_right`: each block is symmetric with a positive diagonal that exceeds the sum of magnitudes of its row's other entries. `root_left`: each block is symmetric with a positive diagonal that exceeds the sum of magnitudes of its row's other entries. `root_right`: each block is symmetric with a positive diagonal that exceeds the sum of magnitudes of its row's other entries.
All inputs are finite; a program needn't handle non-finite values.
Results may differ from a plain program's by a relative error of at most 0.0053.
Values may be sent and summed in bfloat16 or wider, within the bound.
No kernel may reach another device: no remote copies, remote signals or barrier semaphores. Data moves between devices by JAX's collectives and lax.ppermute only.
A program may use at most 128 MiB of HBM per device.

v0:
```python
import jax
import jax.numpy as jnp
from jax import lax
from jax.sharding import PartitionSpec as P

ITERS = 2


ridge_value = 0.001
keep_share = 0.75
step_size = 0.003
graft_floor = 1e-06


def matmul(first, second):
    return jnp.dot(
        first, second, precision=lax.Precision.HIGHEST, preferred_element_type=jnp.float32
    )


def inverse_root(statistic, turns):
    block_size = statistic.shape[-1]
    identity_matrix = jnp.eye(block_size, dtype=jnp.float32)
    shifted = statistic + ridge_value * identity_matrix
    norm_scale = jnp.sqrt(jnp.sum(shifted * shifted))
    current = shifted / norm_scale
    result = identity_matrix * norm_scale ** (-0.25)
    for iteration in range(turns):
        factor = (5.0 * identity_matrix - current) / 4.0
        result = matmul(result, factor)
        square = matmul(factor, factor)
        fourth = matmul(square, square)
        current = matmul(fourth, current)
    return result


def body(hidden, weight, gradient, stats_left, stats_right, root_left, root_right, due_rows):
    block_size = gradient.shape[0]
    gathered = lax.all_gather(hidden, "rep", axis=1, tiled=True)
    gram_left = jnp.dot(gradient, gradient.T, preferred_element_type=jnp.float32) / block_size
    gram_right = jnp.dot(gradient.T, gradient, preferred_element_type=jnp.float32) / block_size
    new_left = keep_share * stats_left + (1.0 - keep_share) * gram_left
    new_right = keep_share * stats_right + (1.0 - keep_share) * gram_right
    row_index = lax.axis_index("fsdp")
    col_index = lax.axis_index("rep")
    half_rows = lax.axis_size("fsdp") // 2
    table_rows = lax.broadcasted_iota(jnp.int32, due_rows.shape, 0)
    table_cols = lax.broadcasted_iota(jnp.int32, due_rows.shape, 1)
    chosen = jnp.sum(
        jnp.where((table_rows == row_index % half_rows) & (table_cols == col_index), due_rows, 0)
    )
    is_due = chosen == row_index
    fresh_left = inverse_root(new_left, ITERS)
    fresh_right = inverse_root(new_right, ITERS)
    left_used = jnp.where(is_due, fresh_left, root_left)
    right_used = jnp.where(is_due, fresh_right, root_right)
    gradient_wide = gradient.astype(jnp.float32)
    conditioned = matmul(matmul(left_used, gradient_wide), right_used)
    graft = jnp.sqrt(jnp.mean(gradient_wide * gradient_wide)) / jnp.sqrt(
        jnp.mean(conditioned * conditioned) + graft_floor
    )
    update = (conditioned * graft).astype(jnp.bfloat16)
    stored = lax.optimization_barrier(update)
    new_weight = (weight.astype(jnp.float32) - step_size * stored.astype(jnp.float32)).astype(
        jnp.bfloat16
    )
    summed = jnp.dot(
        gathered,
        lax.all_gather(new_weight, "fsdp", axis=0, tiled=True),
        preferred_element_type=jnp.float32,
    )
    projected = summed.astype(jnp.bfloat16)
    return (new_left, new_right, update, projected)


def solution(mesh):
    return jax.shard_map(
        body,
        mesh=mesh,
        in_specs=(
            P("fsdp", "rep"),
            P("fsdp", "rep"),
            P("fsdp", "rep"),
            P("fsdp", "rep"),
            P("fsdp", "rep"),
            P("fsdp", "rep"),
            P("fsdp", "rep"),
            P(),
        ),
        out_specs=(P("fsdp", "rep"), P("fsdp", "rep"), P("fsdp", "rep"), P("fsdp", "rep")),
        check_vma=False,
    )
```

profile of v0, /device:TPU:96, one launch (start us, length us, event | category | flops | bytes accessed | tf_op | source)
XLA Modules:
  0.0 209.8 jit_solution(16714306216007861563)
XLA Ops:
  7.2 0.0 all-gather.5.cloned.1.call-start
  7.2 0.7 all-gather.5.cloned.1.call-update
  7.9 0.0 all-gather.3.cloned.1.call-start
  8.0 1.4 select_reduce_fusion
  10.1 2.8 %multiply_reduce_fusion.2 = (f32[]{:T(128)}, f32[512,512]{1,0:T(8,128)S(1)}) fusion(bf16[512,512]{1,0:T(8,128)(2,1)} %param.10, f32[512,512]{1,0:T(8,128)} %param.12), kind=kOutput, calls=%fused_computation.24 | convolution fusion | flops 270532608 | bytes 2621444 | tf_op jit(solution)/shard_map/dot_general | solution.py:41
  13.6 3.6 %multiply_reduce_fusion.3 = (f32[]{:T(128)}, f32[512,512]{1,0:T(8,128)}) fusion(bf16[512,512]{1,0:T(8,128)(2,1)} %param.10, f32[512,512]{1,0:T(8,128)} %param.11), kind=kOutput, calls=%fused_computation.27 | convolution fusion | flops 270532608 | bytes 2621444 | tf_op jit(solution)/shard_map/dot_general | solution.py:40
  18.0 3.6 %fusion.16 = f32[512,512]{1,0:T(8,128)S(1)} fusion(f32[512,512]{1,0:T(8,128)} %get-tuple-element.9, f32[]{:T(128)S(6)} %sqrt.12), kind=kOutput, calls=%fused_computation.32 | convolution fusion | flops 1612447744 | bytes 2097156 | tf_op jit(solution)/shard_map/dot_general | solution.py:16
  21.6 1.8 fusion.51
  23.4 3.2 %fusion.9 = f32[512,512]{1,0:T(8,128)S(1)} fusion(f32[]{:T(128)S(6)} %pow.6, f32[512,512]{1,0:T(8,128)} %get-tuple-element.9, f32[]{:T(128)S(6)} %sqrt.12), kind=kOutput, calls=%fused_computation.25 | convolution fusion | flops 1612972032 | bytes 2097160 | tf_op jit(solution)/shard_map/dot_general | solution.py:16
  26.7 3.2 %fusion.2 = f32[512,512]{1,0:T(8,128)S(1)} fusion(f32[512,512]{1,0:T(8,128)S(1)} %fusion.51, f32[512,512]{1,0:T(8,128)} %get-tuple-element.9, f32[]{:T(128)S(6)} %sqrt.12), kind=kOutput, calls=%fused_computation.10 | convolution fusion | flops 1612709888 | bytes 3145732 | tf_op jit(solution)/shard_map/dot_general | solution.py:16
  29.9 1.8 convolution_select_fusion.1
  31.8 1.0 fusion.52
  32.8 2.2 %fusion.13 = f32[512,512]{1,0:T(8,128)S(1)} fusion(f32[512,512]{1,0:T(8,128)S(1)} %get-tuple-element.11, f32[]{:T(128)S(6)} %sqrt.13), kind=kOutput, calls=%fused_computation.31 | convolution fusion | flops 1612447744 | bytes 2097156 | tf_op jit(solution)/shard_map/dot_general | solution.py:16
  35.0 1.8 fusion.53
  36.8 1.9 fusion.7
  38.8 1.9 fusion.3
  40.7 1.8 convolution_select_fusion
  42.5 2.6 %multiply_reduce_fusion = (f32[]{:T(128)}, f32[512,512]{1,0:T(8,128)S(1)}) fusion(f32[512,512]{1,0:T(8,128)S(1)} %fusion.52, f32[512,512]{1,0:T(8,128)S(1)} %convolution_select_fusion), kind=kOutput, calls=%fused_computation.20 | convolution fusion | flops 1611137024 | bytes 3145732 | tf_op jit(solution)/shard_map/dot_general | solution.py:16
  45.8 0.9 multiply_reduce_fusion.1
  47.4 0.1 multiply_convert_fusion
  47.5 1.0 subtract_convert_fusion
  48.5 141.9 %all-gather.3.cloned.1.call-done = bf16[16384,512]{1,0:T(8,128)(2,1)} async-done(((bf16[512,512]{1,0:T(8,128)(2,1)}), bf16[16384,512]{1,0:T(8,128)(2,1)}) %all-gather.3.cloned.1.call-update) | async-done | bytes 16777232 | tf_op jit(solution)/shard_map/all_gather | solution.py:69
  190.4 11.7 %fusion.4 = bf16[128,512]{0,1:T(8,128)(2,1)S(1)} fusion(bf16[16384,512]{1,0:T(8,128)(2,1)} %all-gather.3.cloned.1.call-done, bf16[128,16384]{1,0:T(8,128)(2,1)} %all-gather.5.cloned.1.call-done), kind=kOutput, calls=%fused_computation.15 | convolution fusion | flops 2147549184 | bytes 21102592 | tf_op jit(solution)/shard_map/dot_general | solution.py:67
  202.2 0.8 copy.12
  (16 shorter events, 0.1 us)
Async XLA Ops:
  7.2 22.7 %copy-start.2 = (f32[512,512]{1,0:T(8,128)S(1)}, f32[512,512]{1,0:T(8,128)}, u32[]{:S(2)}) copy-start(f32[512,512]{1,0:T(8,128)} %param.13) | copy-start | bytes 3145732
  7.2 41.3 %all-gather.5.cloned.1.call-start = ((), (), s32[]{:S(2)}) async-start(), calls=%async_computation.1 | async-start | bytes 4718592 | tf_op jit(solution)/shard_map/all_gather | solution.py:39
  7.9 182.5 %all-gather.3.cloned.1.call-start = ((), (), s32[]{:S(2)}) async-start(), calls=%async_computation | async-start | bytes 17301504 | tf_op jit(solution)/shard_map/all_gather | solution.py:69
  10.0 21.7 %copy-start = (bf16[512,512]{1,0:T(8,128)(2,1)S(1)}, bf16[512,512]{1,0:T(8,128)(2,1)}, u32[]{:S(2)}) copy-start(bf16[512,512]{1,0:T(8,128)(2,1)} %param.10) | copy-start | bytes 1572868
  12.9 25.9 %copy-start.5 = (f32[512,512]{1,0:T(8,128)}, f32[512,512]{1,0:T(8,128)S(1)}, u32[]{:S(2)}) copy-start(f32[512,512]{1,0:T(8,128)S(1)} %get-tuple-element.11) | copy-start | bytes 3145732
  26.7 14.0 %copy-start.3 = (f32[512,512]{1,0:T(8,128)S(1)}, f32[512,512]{1,0:T(8,128)}, u32[]{:S(2)}) copy-start(f32[512,512]{1,0:T(8,128)} %param.14) | copy-start | bytes 3145732
  31.8 15.7 %copy-start.4 = (bf16[512,512]{1,0:T(8,128)(2,1)S(1)}, bf16[512,512]{1,0:T(8,128)(2,1)}, u32[]{:S(2)}) copy-start(bf16[512,512]{1,0:T(8,128)(2,1)} %param.9) | copy-start | bytes 1572868
  47.5 154.7 %copy-start.1 = (bf16[512,512]{1,0:T(8,128)(2,1)}, bf16[512,512]{1,0:T(8,128)(2,1)S(1)}, u32[]{:S(2)}) copy-start(bf16[512,512]{1,0:T(8,128)(2,1)S(1)} %multiply_convert_fusion) | copy-start | bytes 1572868
Sparse Core Ops, SparseCore 0:
  9.8 36.5 all-gather.4
  49.0 141.3 all-gather.2
where the time goes:
time: 212 us; the launch traced here: 210 us
  waiting for transfers between devices  143 us (67%)
  matrix products  45.1 us (21%)
  between operations  17.8 us (8%)
  other arithmetic  3.35 us (2%)
    all_gather x1, waiting for transfers between devices, body(): lax.all_gather(new_weight, 'fsdp', axis=0, tiled=True)  142 us
    dot_general x12, matrix products, matmul(): jnp.dot(first, second, precision=lax.Precision.HIGHEST, preferred_element...  27 us
    dot_general x1, matrix products, body(): jnp.dot(gathered, lax.all_gather(new_weight, 'fsdp', axis=0, tiled=True),...  11.7 us
  transfers between devices with their start and end apart: 2, of which 1 were waited for; matrix products, arithmetic and copies ran while one was open for 18% of the time, Pallas kernels for 0%

commit v1 on v0

v1 whole, which is shorter than its diff:
```python
import jax
import jax.numpy as jnp
from jax import lax
from jax.experimental import pallas as pl
from jax.experimental.pallas import tpu as pltpu
from jax.sharding import Mesh, PartitionSpec as P

BLOCK = 512
ROWS = 128
RIDGE = 0.001
KEEP = 0.75
STEP = 0.003
FLOOR = 1e-06
F32 = jnp.float32
BF16 = jnp.bfloat16
HBM = pl.BlockSpec(memory_space=pltpu.HBM)
VMEM = pl.BlockSpec(memory_space=pltpu.VMEM)


def vmem(one):
    return pltpu.with_memory_space_constraint(one, pltpu.VMEM)


def hbm(one):
    return pltpu.with_memory_space_constraint(one, pltpu.HBM)


def mm(first, second):
    return jnp.dot(first, second, preferred_element_type=F32)


def diagonal_mask():
    rows = lax.broadcasted_iota(jnp.int32, (BLOCK, BLOCK), 0)
    cols = lax.broadcasted_iota(jnp.int32, (BLOCK, BLOCK), 1)
    return rows == cols


def total(values):
    return jnp.sum(jnp.sum(values, axis=0, keepdims=True), axis=1, keepdims=True)


def fresh_root(statistic):
    on_diagonal = diagonal_mask()
    shifted = statistic + jnp.where(on_diagonal, RIDGE, 0.0)
    norm = jnp.sqrt(total(shifted * shifted))
    e1 = shifted * (0.2 / norm)
    e1_low = e1.astype(BF16)
    e2 = mm(e1_low, e1_low)
    e3 = mm(e2.astype(BF16), e1_low)
    e3_low = e3.astype(BF16)
    tail = mm(e3_low, (5.0 * e2 - 10.0 * e1 - e3).astype(BF16))
    a, b = 1.25**2, 1.25**6
    series = -(a + b) * e1 + (5.0 * b) * e2 - (10.0 * b) * e3 - b * tail
    return (series + jnp.where(on_diagonal, a, 0.0)) * lax.rsqrt(jnp.sqrt(norm))


def step_kernel(
    due_hbm, grad_hbm, weight_hbm, sl_hbm, sr_hbm, rl_hbm, rr_hbm,
    nl_hbm, nr_hbm, update_ref, new_ref,
    due_ref, grad_ref, weight_ref, sl, sr, left, right, sems,
):
    copy = pltpu.make_async_copy
    get_due = copy(due_hbm, due_ref, sems.at[0])
    get_grad = copy(grad_hbm, grad_ref, sems.at[1])
    get_weight = copy(weight_hbm, weight_ref, sems.at[2])
    get_sl = copy(sl_hbm, sl, sems.at[3])
    get_sr = copy(sr_hbm, sr, sems.at[4])
    get_rl = copy(rl_hbm, left, sems.at[5])
    get_rr = copy(rr_hbm, right, sems.at[6])
    put_sl = copy(sl, nl_hbm, sems.at[7])
    put_sr = copy(sr, nr_hbm, sems.at[8])
    get_due.start()
    get_grad.start()
    get_sl.start()
    get_sr.start()
    get_weight.start()
    row = lax.axis_index("x") * 8 + lax.axis_index("z")
    col = lax.axis_index("y") * 2 + lax.axis_index("core")
    get_due.wait()
    due = due_ref[col, row % 16] == row

    @pl.when(jnp.logical_not(due))
    def _():
        get_rl.start()
        get_rr.start()

    get_grad.wait()
    grad = grad_ref[...]
    scale = (1.0 - KEEP) / BLOCK
    gram = lax.dot_general(grad, grad, (((1,), (1,)), ((), ())), preferred_element_type=F32)
    get_sl.wait()
    sl[...] = KEEP * sl[...] + scale * gram
    put_sl.start()
    gram = lax.dot_general(grad, grad, (((0,), (0,)), ((), ())), preferred_element_type=F32)
    get_sr.wait()
    sr[...] = KEEP * sr[...] + scale * gram
    put_sr.start()

    @pl.when(due)
    def _():
        left[...] = fresh_root(sl[...])
        right[...] = fresh_root(sr[...])

    @pl.when(jnp.logical_not(due))
    def _():
        get_rl.wait()
        get_rr.wait()

    on_diagonal = diagonal_mask()
    wide = grad.astype(F32)
    used = left[...]
    diag = jnp.sum(jnp.where(on_diagonal, used, 0.0), axis=1, keepdims=True)
    half = diag * wide + mm(jnp.where(on_diagonal, 0.0, used).astype(BF16), grad)
    used = right[...]
    diag = jnp.sum(jnp.where(on_diagonal, used, 0.0), axis=0, keepdims=True)
    cond = half * diag + mm(half.astype(BF16), jnp.where(on_diagonal, 0.0, used).astype(BF16))
    count = 1.0 / (BLOCK * BLOCK)
    graft = jnp.sqrt(total(wide * wide) * count) / jnp.sqrt(total(cond * cond) * count + FLOOR)
    update = (cond * graft).astype(BF16)
    update_ref[...] = update
    get_weight.wait()
    new_ref[...] = (weight_ref[...].astype(F32) - STEP * update.astype(F32)).astype(BF16)
    put_sl.wait()
    put_sr.wait()


def block_step(*operands):
    wide = jax.ShapeDtypeStruct((BLOCK, BLOCK), F32)
    low = jax.ShapeDtypeStruct((BLOCK, BLOCK), BF16)
    return pl.pallas_call(
        step_kernel,
        out_shape=(wide, wide, low, pltpu.VMEM((BLOCK, BLOCK), BF16)),
        in_specs=[HBM] * 7,
        out_specs=(HBM, HBM, VMEM, VMEM),
        scratch_shapes=[pltpu.SMEM((8, 16), jnp.int32)]
        + [pltpu.VMEM((BLOCK, BLOCK), BF16) for _ in range(2)]
        + [pltpu.VMEM((BLOCK, BLOCK), F32) for _ in range(4)]
        + [pltpu.SemaphoreType.DMA((9,))],
        compiler_params=pltpu.CompilerParams(vmem_limit_bytes=24 * 1024 * 1024),
        cost_estimate=pl.CostEstimate(
            flops=2 * 30 * BLOCK**3, bytes_accessed=9 * 1024 * 1024, transcendentals=0
        ),
        name="block_step",
    )(*[hbm(one) for one in operands])


def split_kernel(hidden, *outs):
    place = lax.axis_index("z") % 4
    for shift in range(4):
        start = pl.multiple_of(((place + shift) % 4) * BLOCK, BLOCK)
        outs[shift][...] = hidden[:, pl.ds(start, BLOCK)]


def split_hidden(hidden):
    part = pltpu.VMEM((ROWS, BLOCK), BF16)
    return pl.pallas_call(
        split_kernel,
        out_shape=(part,) * 4,
        in_specs=[VMEM],
        out_specs=(VMEM,) * 4,
        compiler_params=pltpu.CompilerParams(vmem_limit_bytes=4 * 1024 * 1024),
        cost_estimate=pl.CostEstimate(flops=0, bytes_accessed=1024 * 1024, transcendentals=0),
        name="split_hidden",
    )(hidden)


def project_kernel(*refs):
    near, far, weights, outs = refs[0:4], refs[4:8], refs[8:12], refs[12:20]
    placed, sems = refs[20:22]
    x, z = lax.axis_index("x"), lax.axis_index("z")
    y, core = lax.axis_index("y"), lax.axis_index("core")
    copies = [
        pltpu.make_async_copy(weights[i], placed.at[(x + i) % 4], sems.at[i]) for i in range(4)
    ]
    for one in copies:
        one.start()
    for one in copies:
        one.wait()
    sides = []
    for blocks in (near, far):
        acc = mm(blocks[0][...], placed[y])
        for j in range(1, 4):
            acc += mm(blocks[j][...], placed[(y + j) % 4])
        sides.append(acc)
    for s in range(8):
        piece = -s % 4
        rows = slice(piece * ROWS, (piece + 1) * ROWS)
        is_near = ((z + s) % 8) // 4 == core
        outs[s][...] = jnp.where(is_near, sides[0][rows], sides[1][rows]).astype(outs[s].dtype)


def project(near, far, weights):
    part = pltpu.VMEM((ROWS, BLOCK), BF16)
    return pl.pallas_call(
        project_kernel,
        out_shape=(pltpu.VMEM((ROWS, BLOCK), F32),) + (part,) * 7,
        in_specs=[VMEM] * 12,
        out_specs=(VMEM,) * 8,
        scratch_shapes=[pltpu.VMEM((4, BLOCK, BLOCK), BF16), pltpu.SemaphoreType.DMA((4,))],
        compiler_params=pltpu.CompilerParams(vmem_limit_bytes=20 * 1024 * 1024),
        cost_estimate=pl.CostEstimate(
            flops=2 * 1024 * 2048 * BLOCK, bytes_accessed=8 * 1024 * 1024, transcendentals=0
        ),
        name="project",
    )(*[vmem(one) for one in (*near, *far, *weights)])


def ring(size, shift):
    return [((i + shift) % size, i) for i in range(size)]


def body(hidden, weight, gradient, stats_left, stats_right, root_left, root_right, due_rows):
    pieces = split_hidden(hidden)
    tokens = []
    for shift in range(4):
        perm = []
        for z in range(8):
            for core in range(2):
                perm.append((z * 2 + core, (core * 4 + (z % 4 + shift) % 4) * 2 + z // 4))
        tokens.append(lax.ppermute(pieces[shift], ("z", "core"), perm))
    new_left, new_right, update, new_weight = block_step(
        due_rows.T, gradient, weight, stats_left, stats_right, root_left, root_right
    )
    *tokens, new_weight = lax.optimization_barrier((*tokens, new_weight))
    own = jnp.concatenate(tokens, axis=0)
    near = [own] + [lax.ppermute(own, "y", ring(4, j)) for j in (1, 2, 3)]
    weights = [new_weight] + [lax.ppermute(new_weight, "x", ring(4, i)) for i in (1, 2, 3)]
    far = [lax.ppermute(one, "core", ring(2, 1)) for one in near]
    parts = project(near, far, weights)
    projected = parts[0]
    for s in (4, 3, 5, 2, 6, 1, 7):
        projected += lax.ppermute(parts[s], "z", ring(8, 8 - s)).astype(F32)
    return (new_left, new_right, update, projected.astype(BF16))


def solution(mesh):
    grid = Mesh(mesh.devices.reshape(4, 8, 4, 2), ("x", "z", "y", "core"))
    spec = P(("x", "z"), ("y", "core"))
    return jax.shard_map(
        body,
        mesh=grid,
        in_specs=(spec,) * 7 + (P(),),
        out_specs=(spec,) * 4,
        check_vma=False,
    )
```

time: 212 us -> 91.7 us (0.43)
  the two profiles are of different devices: /device:TPU:96 before, /device:TPU:22 now
where the time goes in v1:
time: 91.7 us; the launch traced here: 91.8 us
  waiting for transfers between devices  44 us (48%)
  starting transfers between devices  37.9 us (41%)
  Pallas kernels  7.31 us (8%)
  local copies, waits for them, and re-layouts  1.08 us (1%)
    ppermute x3, waiting for transfers between devices, body(): near = [own] + [lax.ppermute(own, 'y', ring(4, j)) for j in (1, 2, 3)]  20.3 us
    ppermute x7, starting transfers between devices, body(): projected += lax.ppermute(parts[s], 'z', ring(8, 8 - s)).astype(F32)  17.6 us
    ppermute x7, waiting for transfers between devices, body(): projected += lax.ppermute(parts[s], 'z', ring(8, 8 - s)).astype(F32)  12.4 us
    ppermute x3, waiting for transfers between devices, body(): lax.ppermute(new_weight, 'x', ring(4, i))  8.05 us
    ppermute x4, starting transfers between devices, body(): tokens.append(lax.ppermute(pieces[shift], ('z', 'core'), perm))  6.94 us
    ppermute x4, starting transfers between devices, body(): far = [lax.ppermute(one, 'core', ring(2, 1)) for one in near]  6.69 us
    pallas_call x1, Pallas kernels, block_step(): pl.pallas_call(step_kernel, out_shape=(wide, wide, low, pltpu.VMEM((BLOCK...  4.72 us
    ppermute x3, starting transfers between devices, body(): lax.ppermute(new_weight, 'x', ring(4, i))  3.73 us
  transfers between devices with their start and end apart: 21, of which 8 were waited for; matrix products, arithmetic and copies ran while one was open for 0% of the time, Pallas kernels for 5%

profile of v1, /device:TPU:22, one launch (start us, length us, event | category | flops | bytes accessed | tf_op | source)
XLA Modules:
  0.0 91.8 jit_solution(11367526436585163897)
XLA Ops:
  0.6 1.0 %copy-done = bf16[128,2048]{1,0:T(8,128)(2,1)S(1)} copy-done((bf16[128,2048]{1,0:T(8,128)(2,1)S(1)}, bf16[128,2048]{1,0:T(8,128)(2,1)}, u32[]{:S(2)}) %copy-start) | copy-done | bytes 524312
  2.4 2.0 %collective-permute-start.1 = (bf16[128,512]{1,0:T(8,128)(2,1)S(1)}, bf16[128,512]{1,0:T(8,128)(2,1)S(1)}, u32[]{:S(2)}, u32[]{:S(2)}) collective-permute-start(bf16[128,512]{1,0:T(8,128)(2,1)S(1)} %get-tuple-element.29), channel_id=1, source_target_pairs={{0,8},{1,40},{8,16},{9,48},{16,24},{17,56},{24,0},{25,32},{32,9},{... | collective-permute-start | bytes 393224 | tf_op jit(solution)/shard_map/ppermute | solution.py:220
  4.4 3.3 %collective-permute-start.2 = (bf16[128,512]{1,0:T(8,128)(2,1)S(1)}, bf16[128,512]{1,0:T(8,128)(2,1)S(1)}, u32[]{:S(2)}, u32[]{:S(2)}) collective-permute-start(bf16[128,512]{1,0:T(8,128)(2,1)S(1)} %get-tuple-element.30), channel_id=1, source_target_pairs={{0,16},{1,48},{8,24},{9,56},{16,0},{17,32},{24,8},{25,40},{32,17},... | collective-permute-start | bytes 393224 | tf_op jit(solution)/shard_map/ppermute | solution.py:220
  7.7 1.0 %collective-permute-start.3 = (bf16[128,512]{1,0:T(8,128)(2,1)S(1)}, bf16[128,512]{1,0:T(8,128)(2,1)S(1)}, u32[]{:S(2)}, u32[]{:S(2)}) collective-permute-start(bf16[128,512]{1,0:T(8,128)(2,1)S(1)} %get-tuple-element.31), channel_id=1, source_target_pairs={{0,24},{1,56},{8,0},{9,32},{16,8},{17,40},{24,16},{25,48},{32,25},... | collective-permute-start | bytes 393224 | tf_op jit(solution)/shard_map/ppermute | solution.py:220
  8.7 4.7 %block_step.1 = (f32[512,512]{1,0:T(8,128)}, f32[512,512]{1,0:T(8,128)}, bf16[512,512]{1,0:T(8,128)(2,1)}, bf16[512,512]{1,0:T(8,128)(2,1)S(1)}) custom-call(s32[8,16]{1,0:T(8,128)} %bitcast.1, bf16[512,512]{1,0:T(8,128)(2,1)} %grad_hbm.1, bf16[512,512]{1,0:T(8,128)(2,1)} %weight_hbm.1, f32[512,512]{1,0:T(8,128)} %sl_hbm.1, f32[512,512]{1,0:T(8,128)} %sr_hbm.1, ...), custom_call_target="tpu_custom_call" | custom-call | flops 8053063680 | bytes 9437184 | tf_op jit(solution)/shard_map/block_step/pallas_call | solution.py:130
  13.4 3.3 %collective-permute-done.3 = bf16[128,512]{1,0:T(8,128)(2,1)S(1)} collective-permute-done((bf16[128,512]{1,0:T(8,128)(2,1)S(1)}, bf16[128,512]{1,0:T(8,128)(2,1)S(1)}, u32[]{:S(2)}, u32[]{:S(2)}) %collective-permute-start.3) | collective-permute-done | bytes 131104 | tf_op jit(solution)/shard_map/ppermute | solution.py:220
  16.8 6.2 %collective-permute-start.7 = (bf16[512,512]{1,0:T(8,128)(2,1)S(1)}, bf16[512,512]{1,0:T(8,128)(2,1)S(1)}, u32[]{:S(2)}, u32[]{:S(2)}) collective-permute-start(bf16[512,512]{1,0:T(8,128)(2,1)S(1)} %constant_dynamic-update-slice_fusion.refs_0_), channel_id=1, source_target_pairs={{1,0},{0,1},{3,2},{2,3},{5,4},{4,5},{7,6},{6,7},{9,8},{8,9},{11,10... | collective-permute-start | bytes 1572872 | tf_op jit(solution)/shard_map/ppermute | solution.py:228
  22.9 1.3 %collective-permute-start.6 = (bf16[512,512]{1,0:T(8,128)(2,1)S(1)}, bf16[512,512]{1,0:T(8,128)(2,1)S(1)}, u32[]{:S(2)}, u32[]{:S(2)}) collective-permute-start(bf16[512,512]{1,0:T(8,128)(2,1)S(1)} %constant_dynamic-update-slice_fusion.refs_0_), channel_id=1, source_target_pairs={{6,0},{0,2},{2,4},{4,6},{7,1},{1,3},{3,5},{5,7},{14,8},{8,10},{10,... | collective-permute-start | bytes 1572872 | tf_op jit(solution)/shard_map/ppermute | solution.py:226
  24.9 1.1 %collective-permute-start.4 = (bf16[512,512]{1,0:T(8,128)(2,1)S(1)}, bf16[512,512]{1,0:T(8,128)(2,1)S(1)}, u32[]{:S(2)}, u32[]{:S(2)}) collective-permute-start(bf16[512,512]{1,0:T(8,128)(2,1)S(1)} %constant_dynamic-update-slice_fusion.refs_0_), channel_id=1, source_target_pairs={{2,0},{4,2},{6,4},{0,6},{3,1},{5,3},{7,5},{1,7},{10,8},{12,10},{14... | collective-permute-start | bytes 1572872 | tf_op jit(solution)/shard_map/ppermute | solution.py:226
  26.4 2.4 %collective-permute-start.12 = (bf16[512,512]{1,0:T(8,128)(2,1)S(1)}, bf16[512,512]{1,0:T(8,128)(2,1)S(1)}, u32[]{:S(2)}, u32[]{:S(2)}) collective-permute-start(bf16[512,512]{1,0:T(8,128)(2,1)S(1)} %get-tuple-element.37.refs_8_), channel_id=1, source_target_pairs={{128,0},{192,64},{0,128},{64,192},{129,1},{193,65},{1,129},{65,193... | collective-permute-start | bytes 1572872 | tf_op jit(solution)/shard_map/ppermute | solution.py:227
  28.8 19.3 %collective-permute-done.6.refs_3_ = bf16[512,512]{1,0:T(8,128)(2,1)S(1)} collective-permute-done((bf16[512,512]{1,0:T(8,128)(2,1)S(1)}, bf16[512,512]{1,0:T(8,128)(2,1)S(1)}, u32[]{:S(2)}, u32[]{:S(2)}) %collective-permute-start.6) | collective-permute-done | bytes 524320 | tf_op jit(solution)/shard_map/ppermute | solution.py:226
  48.9 1.0 %collective-permute-done.4.refs_1_ = bf16[512,512]{1,0:T(8,128)(2,1)S(1)} collective-permute-done((bf16[512,512]{1,0:T(8,128)(2,1)S(1)}, bf16[512,512]{1,0:T(8,128)(2,1)S(1)}, u32[]{:S(2)}, u32[]{:S(2)}) %collective-permute-start.4) | collective-permute-done | bytes 524320 | tf_op jit(solution)/shard_map/ppermute | solution.py:226
  50.5 8.0 %collective-permute-done.11.refs_9_ = bf16[512,512]{1,0:T(8,128)(2,1)S(1)} collective-permute-done((bf16[512,512]{1,0:T(8,128)(2,1)S(1)}, bf16[512,512]{1,0:T(8,128)(2,1)S(1)}, u32[]{:S(2)}, u32[]{:S(2)}) %collective-permute-start.11) | collective-permute-done | bytes 524320 | tf_op jit(solution)/shard_map/ppermute | solution.py:227
  58.5 2.5 %project.1 = (f32[128,512]{1,0:T(8,128)S(1)}, bf16[128,512]{1,0:T(8,128)(2,1)S(1)}, bf16[128,512]{1,0:T(8,128)(2,1)S(1)}, bf16[128,512]{1,0:T(8,128)(2,1)S(1)}, ...) custom-call(bf16[512,512]{1,0:T(8,128)(2,1)S(1)} %constant_dynamic-u, ...), custom_call_target="tpu_custom_call" | custom-call | flops 2147483648 | bytes 8388608 | tf_op jit(solution)/shard_map/project/pallas_call | solution.py:194
  61.1 6.1 %collective-permute-start.14 = (bf16[128,512]{1,0:T(8,128)(2,1)S(1)}, bf16[128,512]{1,0:T(8,128)(2,1)S(1)}, u32[]{:S(2)}, u32[]{:S(2)}) collective-permute-start(bf16[128,512]{1,0:T(8,128)(2,1)S(1)} %get-tuple-element.39), channel_id=1, source_target_pairs={{32,0},{40,8},{48,16},{56,24},{0,32},{8,40},{16,48},{24,56},{33,1}... | collective-permute-start | bytes 393224 | tf_op jit(solution)/shard_map/ppermute | solution.py:232
  67.1 1.3 %collective-permute-start.15 = (bf16[128,512]{1,0:T(8,128)(2,1)S(1)}, bf16[128,512]{1,0:T(8,128)(2,1)S(1)}, u32[]{:S(2)}, u32[]{:S(2)}) collective-permute-start(bf16[128,512]{1,0:T(8,128)(2,1)S(1)} %get-tuple-element.40), channel_id=1, source_target_pairs={{40,0},{48,8},{56,16},{0,24},{8,32},{16,40},{24,48},{32,56},{41,1}... | collective-permute-start | bytes 393224 | tf_op jit(solution)/shard_map/ppermute | solution.py:232
  68.4 3.8 %collective-permute-start.16 = (bf16[128,512]{1,0:T(8,128)(2,1)S(1)}, bf16[128,512]{1,0:T(8,128)(2,1)S(1)}, u32[]{:S(2)}, u32[]{:S(2)}) collective-permute-start(bf16[128,512]{1,0:T(8,128)(2,1)S(1)} %get-tuple-element.41), channel_id=1, source_target_pairs={{24,0},{32,8},{40,16},{48,24},{56,32},{0,40},{8,48},{16,56},{25,1}... | collective-permute-start | bytes 393224 | tf_op jit(solution)/shard_map/ppermute | solution.py:232
  72.2 1.9 %collective-permute-start.17 = (bf16[128,512]{1,0:T(8,128)(2,1)S(1)}, bf16[128,512]{1,0:T(8,128)(2,1)S(1)}, u32[]{:S(2)}, u32[]{:S(2)}) collective-permute-start(bf16[128,512]{1,0:T(8,128)(2,1)S(1)} %get-tuple-element.42), channel_id=1, source_target_pairs={{48,0},{56,8},{0,16},{8,24},{16,32},{24,40},{32,48},{40,56},{49,1}... | collective-permute-start | bytes 393224 | tf_op jit(solution)/shard_map/ppermute | solution.py:232
  74.0 2.3 %collective-permute-start.18 = (bf16[128,512]{1,0:T(8,128)(2,1)S(1)}, bf16[128,512]{1,0:T(8,128)(2,1)S(1)}, u32[]{:S(2)}, u32[]{:S(2)}) collective-permute-start(bf16[128,512]{1,0:T(8,128)(2,1)S(1)} %get-tuple-element.43), channel_id=1, source_target_pairs={{16,0},{24,8},{32,16},{40,24},{48,32},{56,40},{0,48},{8,56},{17,1}... | collective-permute-start | bytes 393224 | tf_op jit(solution)/shard_map/ppermute | solution.py:232
  76.3 2.3 %collective-permute-start.19 = (bf16[128,512]{1,0:T(8,128)(2,1)S(1)}, bf16[128,512]{1,0:T(8,128)(2,1)S(1)}, u32[]{:S(2)}, u32[]{:S(2)}) collective-permute-start(bf16[128,512]{1,0:T(8,128)(2,1)S(1)} %get-tuple-element.44), channel_id=1, source_target_pairs={{56,0},{0,8},{8,16},{16,24},{24,32},{32,40},{40,48},{48,56},{57,1}... | collective-permute-start | bytes 393224 | tf_op jit(solution)/shard_map/ppermute | solution.py:232
  78.6 4.8 %collective-permute-done.15 = bf16[128,512]{1,0:T(8,128)(2,1)S(1)} collective-permute-done((bf16[128,512]{1,0:T(8,128)(2,1)S(1)}, bf16[128,512]{1,0:T(8,128)(2,1)S(1)}, u32[]{:S(2)}, u32[]{:S(2)}) %collective-permute-start.15) | collective-permute-done | bytes 131104 | tf_op jit(solution)/shard_map/ppermute | solution.py:232
  83.4 1.3 %collective-permute-done.16 = bf16[128,512]{1,0:T(8,128)(2,1)S(1)} collective-permute-done((bf16[128,512]{1,0:T(8,128)(2,1)S(1)}, bf16[128,512]{1,0:T(8,128)(2,1)S(1)}, u32[]{:S(2)}, u32[]{:S(2)}) %collective-permute-start.16) | collective-permute-done | bytes 131104 | tf_op jit(solution)/shard_map/ppermute | solution.py:232
  84.7 3.5 %collective-permute-done.17 = bf16[128,512]{1,0:T(8,128)(2,1)S(1)} collective-permute-done((bf16[128,512]{1,0:T(8,128)(2,1)S(1)}, bf16[128,512]{1,0:T(8,128)(2,1)S(1)}, u32[]{:S(2)}, u32[]{:S(2)}) %collective-permute-start.17) | collective-permute-done | bytes 131104 | tf_op jit(solution)/shard_map/ppermute | solution.py:232
  88.2 2.8 %collective-permute-done.20 = bf16[128,512]{1,0:T(8,128)(2,1)S(1)} collective-permute-done((bf16[128,512]{1,0:T(8,128)(2,1)S(1)}, bf16[128,512]{1,0:T(8,128)(2,1)S(1)}, u32[]{:S(2)}, u32[]{:S(2)}) %collective-permute-start.20) | collective-permute-done | bytes 131104 | tf_op jit(solution)/shard_map/ppermute | solution.py:232
  (28 shorter events, 4.0 us)
Async XLA Ops:
  0.6 1.0 %copy-start = (bf16[128,2048]{1,0:T(8,128)(2,1)S(1)}, bf16[128,2048]{1,0:T(8,128)(2,1)}, u32[]{:S(2)}) copy-start(bf16[128,2048]{1,0:T(8,128)(2,1)} %hidden.1) | copy-start | bytes 1572868
  1.7 11.7 %collective-permute-start = (bf16[128,512]{1,0:T(8,128)(2,1)S(1)}, bf16[128,512]{1,0:T(8,128)(2,1)S(1)}, u32[]{:S(2)}, u32[]{:S(2)}) collective-permute-start(bf16[128,512]{1,0:T(8,128)(2,1)S(1)} %get-tuple-element.28), channel_id=1, source_target_pairs={{0,0},{1,32},{8,8},{9,40},{16,16},{17,48},{24,24},{25,56},{32,1},{... | collective-permute-start | bytes 393224 | tf_op jit(solution)/shard_map/ppermute | solution.py:220
  2.4 11.0 %collective-permute-start.1 = (bf16[128,512]{1,0:T(8,128)(2,1)S(1)}, bf16[128,512]{1,0:T(8,128)(2,1)S(1)}, u32[]{:S(2)}, u32[]{:S(2)}) collective-permute-start(bf16[128,512]{1,0:T(8,128)(2,1)S(1)} %get-tuple-element.29), channel_id=1, source_target_pairs={{0,8},{1,40},{8,16},{9,48},{16,24},{17,56},{24,0},{25,32},{32,9},{... | collective-permute-start | bytes 393224 | tf_op jit(solution)/shard_map/ppermute | solution.py:220
  4.4 9.0 %collective-permute-start.2 = (bf16[128,512]{1,0:T(8,128)(2,1)S(1)}, bf16[128,512]{1,0:T(8,128)(2,1)S(1)}, u32[]{:S(2)}, u32[]{:S(2)}) collective-permute-start(bf16[128,512]{1,0:T(8,128)(2,1)S(1)} %get-tuple-element.30), channel_id=1, source_target_pairs={{0,16},{1,48},{8,24},{9,56},{16,0},{17,32},{24,8},{25,40},{32,17},... | collective-permute-start | bytes 393224 | tf_op jit(solution)/shard_map/ppermute | solution.py:220
  7.7 9.0 %collective-permute-start.3 = (bf16[128,512]{1,0:T(8,128)(2,1)S(1)}, bf16[128,512]{1,0:T(8,128)(2,1)S(1)}, u32[]{:S(2)}, u32[]{:S(2)}) collective-permute-start(bf16[128,512]{1,0:T(8,128)(2,1)S(1)} %get-tuple-element.31), channel_id=1, source_target_pairs={{0,24},{1,56},{8,0},{9,32},{16,8},{17,40},{24,16},{25,48},{32,25},... | collective-permute-start | bytes 393224 | tf_op jit(solution)/shard_map/ppermute | solution.py:220
  16.8 9.6 %collective-permute-start.7 = (bf16[512,512]{1,0:T(8,128)(2,1)S(1)}, bf16[512,512]{1,0:T(8,128)(2,1)S(1)}, u32[]{:S(2)}, u32[]{:S(2)}) collective-permute-start(bf16[512,512]{1,0:T(8,128)(2,1)S(1)} %constant_dynamic-update-slice_fusion.refs_0_), channel_id=1, source_target_pairs={{1,0},{0,1},{3,2},{2,3},{5,4},{4,5},{7,6},{6,7},{9,8},{8,9},{11,10... | collective-permute-start | bytes 1572872 | tf_op jit(solution)/shard_map/ppermute | solution.py:228
  22.9 25.2 %collective-permute-start.6 = (bf16[512,512]{1,0:T(8,128)(2,1)S(1)}, bf16[512,512]{1,0:T(8,128)(2,1)S(1)}, u32[]{:S(2)}, u32[]{:S(2)}) collective-permute-start(bf16[512,512]{1,0:T(8,128)(2,1)S(1)} %constant_dynamic-update-slice_fusion.refs_0_), channel_id=1, source_target_pairs={{6,0},{0,2},{2,4},{4,6},{7,1},{1,3},{3,5},{5,7},{14,8},{8,10},{10,... | collective-permute-start | bytes 1572872 | tf_op jit(solution)/shard_map/ppermute | solution.py:226
  24.2 24.7 %collective-permute-start.5 = (bf16[512,512]{1,0:T(8,128)(2,1)S(1)}, bf16[512,512]{1,0:T(8,128)(2,1)S(1)}, u32[]{:S(2)}, u32[]{:S(2)}) collective-permute-start(bf16[512,512]{1,0:T(8,128)(2,1)S(1)} %constant_dynamic-update-slice_fusion.refs_0_), channel_id=1, source_target_pairs={{4,0},{6,2},{0,4},{2,6},{5,1},{7,3},{1,5},{3,7},{12,8},{14,10},{8,... | collective-permute-start | bytes 1572872 | tf_op jit(solution)/shard_map/ppermute | solution.py:226
  24.9 25.1 %collective-permute-start.4 = (bf16[512,512]{1,0:T(8,128)(2,1)S(1)}, bf16[512,512]{1,0:T(8,128)(2,1)S(1)}, u32[]{:S(2)}, u32[]{:S(2)}) collective-permute-start(bf16[512,512]{1,0:T(8,128)(2,1)S(1)} %constant_dynamic-update-slice_fusion.refs_0_), channel_id=1, source_target_pairs={{2,0},{4,2},{6,4},{0,6},{3,1},{5,3},{7,5},{1,7},{10,8},{12,10},{14... | collective-permute-start | bytes 1572872 | tf_op jit(solution)/shard_map/ppermute | solution.py:226
  25.9 24.0 %collective-permute-start.13 = (bf16[512,512]{1,0:T(8,128)(2,1)S(1)}, bf16[512,512]{1,0:T(8,128)(2,1)S(1)}, u32[]{:S(2)}, u32[]{:S(2)}) collective-permute-start(bf16[512,512]{1,0:T(8,128)(2,1)S(1)} %get-tuple-element.37.refs_8_), channel_id=1, source_target_pairs={{192,0},{0,64},{64,128},{128,192},{193,1},{1,65},{65,129},{129,193... | collective-permute-start | bytes 1572872 | tf_op jit(solution)/shard_map/ppermute | solution.py:227
  26.4 24.1 %collective-permute-start.12 = (bf16[512,512]{1,0:T(8,128)(2,1)S(1)}, bf16[512,512]{1,0:T(8,128)(2,1)S(1)}, u32[]{:S(2)}, u32[]{:S(2)}) collective-permute-start(bf16[512,512]{1,0:T(8,128)(2,1)S(1)} %get-tuple-element.37.refs_8_), channel_id=1, source_target_pairs={{128,0},{192,64},{0,128},{64,192},{129,1},{193,65},{1,129},{65,193... | collective-permute-start | bytes 1572872 | tf_op jit(solution)/shard_map/ppermute | solution.py:227
  48.1 10.4 %collective-permute-start.11 = (bf16[512,512]{1,0:T(8,128)(2,1)S(1)}, bf16[512,512]{1,0:T(8,128)(2,1)S(1)}, u32[]{:S(2)}, u32[]{:S(2)}) collective-permute-start(bf16[512,512]{1,0:T(8,128)(2,1)S(1)} %get-tuple-element.37.refs_8_), channel_id=1, source_target_pairs={{64,0},{128,64},{192,128},{0,192},{65,1},{129,65},{193,129},{1,193... | collective-permute-start | bytes 1572872 | tf_op jit(solution)/shard_map/ppermute | solution.py:227
  48.9 9.6 %collective-permute-start.10 = (bf16[512,512]{1,0:T(8,128)(2,1)S(1)}, bf16[512,512]{1,0:T(8,128)(2,1)S(1)}, u32[]{:S(2)}, u32[]{:S(2)}) collective-permute-start(bf16[512,512]{1,0:T(8,128)(2,1)S(1)} %collective-permute-done.6.refs_3_), channel_id=1, source_target_pairs={{1,0},{0,1},{3,2},{2,3},{5,4},{4,5},{7,6},{6,7},{9,8},{8,9},{11,10... | collective-permute-start | bytes 1572872 | tf_op jit(solution)/shard_map/ppermute | solution.py:228
  49.9 8.6 %collective-permute-start.9 = (bf16[512,512]{1,0:T(8,128)(2,1)S(1)}, bf16[512,512]{1,0:T(8,128)(2,1)S(1)}, u32[]{:S(2)}, u32[]{:S(2)}) collective-permute-start(bf16[512,512]{1,0:T(8,128)(2,1)S(1)} %collective-permute-done.5.refs_2_), channel_id=1, source_target_pairs={{1,0},{0,1},{3,2},{2,3},{5,4},{4,5},{7,6},{6,7},{9,8},{8,9},{11,10... | collective-permute-start | bytes 1572872 | tf_op jit(solution)/shard_map/ppermute | solution.py:228
  49.9 8.6 %collective-permute-start.8 = (bf16[512,512]{1,0:T(8,128)(2,1)S(1)}, bf16[512,512]{1,0:T(8,128)(2,1)S(1)}, u32[]{:S(2)}, u32[]{:S(2)}) collective-permute-start(bf16[512,512]{1,0:T(8,128)(2,1)S(1)} %collective-permute-done.4.refs_1_), channel_id=1, source_target_pairs={{1,0},{0,1},{3,2},{2,3},{5,4},{4,5},{7,6},{6,7},{9,8},{8,9},{11,10... | collective-permute-start | bytes 1572872 | tf_op jit(solution)/shard_map/ppermute | solution.py:228
  61.1 15.3 %collective-permute-start.14 = (bf16[128,512]{1,0:T(8,128)(2,1)S(1)}, bf16[128,512]{1,0:T(8,128)(2,1)S(1)}, u32[]{:S(2)}, u32[]{:S(2)}) collective-permute-start(bf16[128,512]{1,0:T(8,128)(2,1)S(1)} %get-tuple-element.39), channel_id=1, source_target_pairs={{32,0},{40,8},{48,16},{56,24},{0,32},{8,40},{16,48},{24,56},{33,1}... | collective-permute-start | bytes 393224 | tf_op jit(solution)/shard_map/ppermute | solution.py:232
  67.1 16.3 %collective-permute-start.15 = (bf16[128,512]{1,0:T(8,128)(2,1)S(1)}, bf16[128,512]{1,0:T(8,128)(2,1)S(1)}, u32[]{:S(2)}, u32[]{:S(2)}) collective-permute-start(bf16[128,512]{1,0:T(8,128)(2,1)S(1)} %get-tuple-element.40), channel_id=1, source_target_pairs={{40,0},{48,8},{56,16},{0,24},{8,32},{16,40},{24,48},{32,56},{41,1}... | collective-permute-start | bytes 393224 | tf_op jit(solution)/shard_map/ppermute | solution.py:232
  68.4 16.3 %collective-permute-start.16 = (bf16[128,512]{1,0:T(8,128)(2,1)S(1)}, bf16[128,512]{1,0:T(8,128)(2,1)S(1)}, u32[]{:S(2)}, u32[]{:S(2)}) collective-permute-start(bf16[128,512]{1,0:T(8,128)(2,1)S(1)} %get-tuple-element.41), channel_id=1, source_target_pairs={{24,0},{32,8},{40,16},{48,24},{56,32},{0,40},{8,48},{16,56},{25,1}... | collective-permute-start | bytes 393224 | tf_op jit(solution)/shard_map/ppermute | solution.py:232
  72.2 16.0 %collective-permute-start.17 = (bf16[128,512]{1,0:T(8,128)(2,1)S(1)}, bf16[128,512]{1,0:T(8,128)(2,1)S(1)}, u32[]{:S(2)}, u32[]{:S(2)}) collective-permute-start(bf16[128,512]{1,0:T(8,128)(2,1)S(1)} %get-tuple-element.42), channel_id=1, source_target_pairs={{48,0},{56,8},{0,16},{8,24},{16,32},{24,40},{32,48},{40,56},{49,1}... | collective-permute-start | bytes 393224 | tf_op jit(solution)/shard_map/ppermute | solution.py:232
  74.0 14.2 %collective-permute-start.18 = (bf16[128,512]{1,0:T(8,128)(2,1)S(1)}, bf16[128,512]{1,0:T(8,128)(2,1)S(1)}, u32[]{:S(2)}, u32[]{:S(2)}) collective-permute-start(bf16[128,512]{1,0:T(8,128)(2,1)S(1)} %get-tuple-element.43), channel_id=1, source_target_pairs={{16,0},{24,8},{32,16},{40,24},{48,32},{56,40},{0,48},{8,56},{17,1}... | collective-permute-start | bytes 393224 | tf_op jit(solution)/shard_map/ppermute | solution.py:232
  76.3 11.9 %collective-permute-start.19 = (bf16[128,512]{1,0:T(8,128)(2,1)S(1)}, bf16[128,512]{1,0:T(8,128)(2,1)S(1)}, u32[]{:S(2)}, u32[]{:S(2)}) collective-permute-start(bf16[128,512]{1,0:T(8,128)(2,1)S(1)} %get-tuple-element.44), channel_id=1, source_target_pairs={{56,0},{0,8},{8,16},{16,24},{24,32},{32,40},{40,48},{48,56},{57,1}... | collective-permute-start | bytes 393224 | tf_op jit(solution)/shard_map/ppermute | solution.py:232
  83.4 7.6 %collective-permute-start.20 = (bf16[128,512]{1,0:T(8,128)(2,1)S(1)}, bf16[128,512]{1,0:T(8,128)(2,1)S(1)}, u32[]{:S(2)}, u32[]{:S(2)}) collective-permute-start(bf16[128,512]{1,0:T(8,128)(2,1)S(1)} %get-tuple-element.45), channel_id=1, source_target_pairs={{8,0},{16,8},{24,16},{32,24},{40,32},{48,40},{56,48},{0,56},{9,1},... | collective-permute-start | bytes 393224 | tf_op jit(solution)/shard_map/ppermute | solution.py:232

commit v2 on v1

--- a/solution.py
+++ b/solution.py
@@ -6,6 +6,7 @@
 from jax.sharding import Mesh, PartitionSpec as P
 
 BLOCK = 512
+HALF = 256
 ROWS = 128
 RIDGE = 0.001
 KEEP = 0.75
@@ -165,13 +166,19 @@
 
 
 def project_kernel(*refs):
-    near, far, weights, outs = refs[0:4], refs[4:8], refs[8:12], refs[12:20]
-    placed, sems = refs[20:22]
+    near, far, weights, outs = refs[0:4], refs[4:8], refs[8:13], refs[13:21]
+    placed, sems = refs[21:23]
     x, z = lax.axis_index("x"), lax.axis_index("z")
     y, core = lax.axis_index("y"), lax.axis_index("core")
-    copies = [
-        pltpu.make_async_copy(weights[i], placed.at[(x + i) % 4], sems.at[i]) for i in range(4)
+    opposite = placed.at[(x + 2) % 4]
+    homes = [
+        placed.at[x],
+        placed.at[(x + 1) % 4],
+        opposite.at[pl.ds(0, HALF)],
+        opposite.at[pl.ds(HALF, HALF)],
+        placed.at[(x + 3) % 4],
     ]
+    copies = [pltpu.make_async_copy(weights[i], homes[i], sems.at[i]) for i in range(5)]
     for one in copies:
         one.start()
     for one in copies:
@@ -194,9 +201,9 @@
     return pl.pallas_call(
         project_kernel,
         out_shape=(pltpu.VMEM((ROWS, BLOCK), F32),) + (part,) * 7,
-        in_specs=[VMEM] * 12,
+        in_specs=[VMEM] * 13,
         out_specs=(VMEM,) * 8,
-        scratch_shapes=[pltpu.VMEM((4, BLOCK, BLOCK), BF16), pltpu.SemaphoreType.DMA((4,))],
+        scratch_shapes=[pltpu.VMEM((4, BLOCK, BLOCK), BF16), pltpu.SemaphoreType.DMA((5,))],
         compiler_params=pltpu.CompilerParams(vmem_limit_bytes=20 * 1024 * 1024),
         cost_estimate=pl.CostEstimate(
             flops=2 * 1024 * 2048 * BLOCK, bytes_accessed=8 * 1024 * 1024, transcendentals=0
@@ -207,6 +214,10 @@
 
 def ring(size, shift):
     return [((i + shift) % size, i) for i in range(size)]
+
+
+def add(first, second):
+    return (first.astype(F32) + second.astype(F32)).astype(BF16)
 
 
 def body(hidden, weight, gradient, stats_left, stats_right, root_left, root_right, due_rows):
@@ -224,12 +235,20 @@
     *tokens, new_weight = lax.optimization_barrier((*tokens, new_weight))
     own = jnp.concatenate(tokens, axis=0)
     near = [own] + [lax.ppermute(own, "y", ring(4, j)) for j in (1, 2, 3)]
-    weights = [new_weight] + [lax.ppermute(new_weight, "x", ring(4, i)) for i in (1, 2, 3)]
-    far = [lax.ppermute(one, "core", ring(2, 1)) for one in near]
+    one, three = (lax.ppermute(new_weight, "x", ring(4, i)) for i in (1, 3))
+    top = lax.ppermute(one[:HALF], "x", ring(4, 1))
+    bottom = lax.ppermute(three[HALF:], "x", ring(4, 3))
+    near[1], top, bottom = lax.optimization_barrier((near[1], top, bottom))
+    weights = [new_weight, one, top, bottom, three]
+    far = [lax.ppermute(piece, "core", ring(2, 1)) for piece in near]
     parts = project(near, far, weights)
-    projected = parts[0]
-    for s in (4, 3, 5, 2, 6, 1, 7):
-        projected += lax.ppermute(parts[s], "z", ring(8, 8 - s)).astype(F32)
+    up, down = parts[3], parts[5]
+    for near_up, near_down in ((parts[2], parts[6]), (parts[1], parts[7])):
+        up = add(near_up, lax.ppermute(up, "z", ring(8, 7)))
+        down = add(near_down, lax.ppermute(down, "z", ring(8, 1)))
+    up, down = lax.ppermute(up, "z", ring(8, 7)), lax.ppermute(down, "z", ring(8, 1))
+    far_sum = lax.ppermute(parts[4], "z", ring(8, 4))
+    projected = parts[0] + up.astype(F32) + down.astype(F32) + far_sum.astype(F32)
     return (new_left, new_right, update, projected.astype(BF16))
 
 

time: 91.7 us -> 79.5 us (0.87)
  the two profiles are of different devices: /device:TPU:22 before, /device:TPU:96 now
where the time goes in v2:
time: 79.5 us; the launch traced here: 79.4 us
  starting transfers between devices  43.6 us (55%)
  waiting for transfers between devices  25.8 us (32%)
  Pallas kernels  7.28 us (9%)
  local copies, waits for them, and re-layouts  1.11 us (1%)
  other arithmetic  0.86 us (1%)
    ppermute x4, starting transfers between devices, body(): far = [lax.ppermute(piece, 'core', ring(2, 1)) for piece in near]  15.8 us
    ppermute x2, starting transfers between devices, body(): up = add(near_up, lax.ppermute(up, 'z', ring(8, 7)))  8.5 us
    ppermute x4, waiting for transfers between devices, body(): tokens.append(lax.ppermute(pieces[shift], ('z', 'core'), perm))  5.65 us
    pallas_call x1, Pallas kernels, block_step(): pl.pallas_call(step_kernel, out_shape=(wide, wide, low, pltpu.VMEM((BLOCK...  4.72 us
    ppermute x3, starting transfers between devices, body(): near = [own] + [lax.ppermute(own, 'y', ring(4, j)) for j in (1, 2, 3)]  4.54 us
    ppermute x2, waiting for transfers between devices, body(): up = add(near_up, lax.ppermute(up, 'z', ring(8, 7)))  4.31 us
    ppermute x1, waiting for transfers between devices, body(): lax.ppermute(down, 'z', ring(8, 1))  3.77 us
    ppermute x1, starting transfers between devices, body(): top = lax.ppermute(one[:HALF], 'x', ring(4, 1))  3.29 us
  transfers between devices with their start and end apart: 22, of which 11 were waited for; matrix products, arithmetic and copies ran while one was open for 0% of the time, Pallas kernels for 6%

profile of v2, /device:TPU:96, one launch (start us, length us, event | category | flops | bytes accessed | tf_op | source)
XLA Modules:
  0.0 79.4 jit_solution(12070265429996659057)
XLA Ops:
  0.6 1.0 %copy-done = bf16[128,2048]{1,0:T(8,128)(2,1)S(1)} copy-done((bf16[128,2048]{1,0:T(8,128)(2,1)S(1)}, bf16[128,2048]{1,0:T(8,128)(2,1)}, u32[]{:S(2)}) %copy-start) | copy-done | bytes 524312
  2.4 1.0 %collective-permute-start.1 = (bf16[128,512]{1,0:T(8,128)(2,1)S(1)}, bf16[128,512]{1,0:T(8,128)(2,1)S(1)}, u32[]{:S(2)}, u32[]{:S(2)}) collective-permute-start(bf16[128,512]{1,0:T(8,128)(2,1)S(1)} %get-tuple-element.32), channel_id=1, source_target_pairs={{0,8},{1,40},{8,16},{9,48},{16,24},{17,56},{24,0},{25,32},{32,9},{... | collective-permute-start | bytes 393224 | tf_op jit(solution)/shard_map/ppermute | solution.py:231
  4.5 4.7 %block_step.1 = (f32[512,512]{1,0:T(8,128)}, f32[512,512]{1,0:T(8,128)}, bf16[512,512]{1,0:T(8,128)(2,1)}, bf16[512,512]{1,0:T(8,128)(2,1)S(1)}) custom-call(s32[8,16]{1,0:T(8,128)} %bitcast.1, bf16[512,512]{1,0:T(8,128)(2,1)} %grad_hbm.1, bf16[512,512]{1,0:T(8,128)(2,1)} %weight_hbm.1, f32[512,512]{1,0:T(8,128)} %sl_hbm.1, f32[512,512]{1,0:T(8,128)} %sr_hbm.1, ...), custom_call_target="tpu_custom_call" | custom-call | flops 8053063680 | bytes 9437184 | tf_op jit(solution)/shard_map/block_step/pallas_call | solution.py:131
  9.2 5.6 %collective-permute-done.2 = bf16[128,512]{1,0:T(8,128)(2,1)S(1)} collective-permute-done((bf16[128,512]{1,0:T(8,128)(2,1)S(1)}, bf16[128,512]{1,0:T(8,128)(2,1)S(1)}, u32[]{:S(2)}, u32[]{:S(2)}) %collective-permute-start.2) | collective-permute-done | bytes 131104 | tf_op jit(solution)/shard_map/ppermute | solution.py:231
  15.0 3.1 %collective-permute-start.5 = (bf16[512,512]{1,0:T(8,128)(2,1)S(1)}, bf16[512,512]{1,0:T(8,128)(2,1)S(1)}, u32[]{:S(2)}, u32[]{:S(2)}) collective-permute-start(bf16[512,512]{1,0:T(8,128)(2,1)S(1)} %get-tuple-element.40.refs_8_), channel_id=1, source_target_pairs={{64,0},{128,64},{192,128},{0,192},{65,1},{129,65},{193,129},{1,193... | collective-permute-start | bytes 1572872 | tf_op jit(solution)/shard_map/ppermute | solution.py:238
  18.5 2.9 %collective-permute-start.9 = (bf16[512,512]{1,0:T(8,128)(2,1)S(1)}, bf16[512,512]{1,0:T(8,128)(2,1)S(1)}, u32[]{:S(2)}, u32[]{:S(2)}) collective-permute-start(bf16[512,512]{1,0:T(8,128)(2,1)S(1)} %constant_dynamic-update-slice_fusion.refs_0_), channel_id=1, source_target_pairs={{4,0},{6,2},{0,4},{2,6},{5,1},{7,3},{1,5},{3,7},{12,8},{14,10},{8,... | collective-permute-start | bytes 1572872 | tf_op jit(solution)/shard_map/ppermute | solution.py:237
  21.4 1.3 %collective-permute-start.4 = (bf16[512,512]{1,0:T(8,128)(2,1)S(1)}, bf16[512,512]{1,0:T(8,128)(2,1)S(1)}, u32[]{:S(2)}, u32[]{:S(2)}) collective-permute-start(bf16[512,512]{1,0:T(8,128)(2,1)S(1)} %constant_dynamic-update-slice_fusion.refs_0_), channel_id=1, source_target_pairs={{2,0},{4,2},{6,4},{0,6},{3,1},{5,3},{7,5},{1,7},{10,8},{12,10},{14... | collective-permute-start | bytes 1572872 | tf_op jit(solution)/shard_map/ppermute | solution.py:237
  22.7 2.5 %collective-permute-done.7.refs_12_ = bf16[512,512]{1,0:T(8,128)(2,1)S(1)} collective-permute-done((bf16[512,512]{1,0:T(8,128)(2,1)S(1)}, bf16[512,512]{1,0:T(8,128)(2,1)S(1)}, u32[]{:S(2)}, u32[]{:S(2)}) %collective-permute-start.7) | collective-permute-done | bytes 524320 | tf_op jit(solution)/shard_map/ppermute | solution.py:238
  25.4 3.3 %collective-permute-start.6 = (bf16[256,512]{1,0:T(8,128)(2,1)S(1)}, bf16[256,512]{1,0:T(8,128)(2,1)S(1)}, u32[]{:S(2)}, u32[]{:S(2)}) collective-permute-start(bf16[256,512]{1,0:T(8,128)(2,1)S(1)} %slice.8), channel_id=1, source_target_pairs={{64,0},{128,64},{192,128},{0,192},{65,1},{129,65},{193,129},{1,193... | collective-permute-start | bytes 786440 | tf_op jit(solution)/shard_map/ppermute | solution.py:239
  28.7 1.8 %collective-permute-done.10.refs_3_ = bf16[512,512]{1,0:T(8,128)(2,1)S(1)} collective-permute-done((bf16[512,512]{1,0:T(8,128)(2,1)S(1)}, bf16[512,512]{1,0:T(8,128)(2,1)S(1)}, u32[]{:S(2)}, u32[]{:S(2)}) %collective-permute-start.10) | collective-permute-done | bytes 524320 | tf_op jit(solution)/shard_map/ppermute | solution.py:237
  30.5 9.2 %collective-permute-start.11 = (bf16[512,512]{1,0:T(8,128)(2,1)S(1)}, bf16[512,512]{1,0:T(8,128)(2,1)S(1)}, u32[]{:S(2)}, u32[]{:S(2)}) collective-permute-start(bf16[512,512]{1,0:T(8,128)(2,1)S(1)} %constant_dynamic-update-slice_fusion.refs_0_), channel_id=1, source_target_pairs={{1,0},{0,1},{3,2},{2,3},{5,4},{4,5},{7,6},{6,7},{9,8},{8,9},{11,10... | collective-permute-start | bytes 1572872 | tf_op jit(solution)/shard_map/ppermute | solution.py:243
  39.7 5.6 %collective-permute-start.14 = (bf16[512,512]{1,0:T(8,128)(2,1)S(1)}, bf16[512,512]{1,0:T(8,128)(2,1)S(1)}, u32[]{:S(2)}, u32[]{:S(2)}) collective-permute-start(bf16[512,512]{1,0:T(8,128)(2,1)S(1)} %collective-permute-done.10.refs_3_), channel_id=1, source_target_pairs={{1,0},{0,1},{3,2},{2,3},{5,4},{4,5},{7,6},{6,7},{9,8},{8,9},{11,10... | collective-permute-start | bytes 1572872 | tf_op jit(solution)/shard_map/ppermute | solution.py:243
  45.3 0.9 %collective-permute-start.13 = (bf16[512,512]{1,0:T(8,128)(2,1)S(1)}, bf16[512,512]{1,0:T(8,128)(2,1)S(1)}, u32[]{:S(2)}, u32[]{:S(2)}) collective-permute-start(bf16[512,512]{1,0:T(8,128)(2,1)S(1)} %collective-permute-done.9.refs_2_), channel_id=1, source_target_pairs={{1,0},{0,1},{3,2},{2,3},{5,4},{4,5},{7,6},{6,7},{9,8},{8,9},{11,10... | collective-permute-start | bytes 1572872 | tf_op jit(solution)/shard_map/ppermute | solution.py:243
  46.9 0.9 %collective-permute-done.13.refs_6_ = bf16[512,512]{1,0:T(8,128)(2,1)S(1)} collective-permute-done((bf16[512,512]{1,0:T(8,128)(2,1)S(1)}, bf16[512,512]{1,0:T(8,128)(2,1)S(1)}, u32[]{:S(2)}, u32[]{:S(2)}) %collective-permute-start.13) | collective-permute-done | bytes 524320 | tf_op jit(solution)/shard_map/ppermute | solution.py:243
  48.5 2.5 %project.1 = (f32[128,512]{1,0:T(8,128)S(1)}, bf16[128,512]{1,0:T(8,128)(2,1)S(1)}, bf16[128,512]{1,0:T(8,128)(2,1)S(1)}, bf16[128,512]{1,0:T(8,128)(2,1)S(1)}, ...) custom-call(bf16[512,512]{1,0:T(8,128)(2,1)S(1)} %constant_dynamic-u, ...), custom_call_target="tpu_custom_call" | custom-call | flops 2147483648 | bytes 8388608 | tf_op jit(solution)/shard_map/project/pallas_call | solution.py:201
  51.1 4.7 %collective-permute-start.15 = (bf16[128,512]{1,0:T(8,128)(2,1)S(1)}, bf16[128,512]{1,0:T(8,128)(2,1)S(1)}, u32[]{:S(2)}, u32[]{:S(2)}) collective-permute-start(bf16[128,512]{1,0:T(8,128)(2,1)S(1)} %get-tuple-element.47), channel_id=1, source_target_pairs={{56,0},{0,8},{8,16},{16,24},{24,32},{32,40},{40,48},{48,56},{57,1}... | collective-permute-start | bytes 393224 | tf_op jit(solution)/shard_map/ppermute | solution.py:247
  55.8 2.2 %collective-permute-start.21 = (bf16[128,512]{1,0:T(8,128)(2,1)S(1)}, bf16[128,512]{1,0:T(8,128)(2,1)S(1)}, u32[]{:S(2)}, u32[]{:S(2)}) collective-permute-start(bf16[128,512]{1,0:T(8,128)(2,1)S(1)} %get-tuple-element.51), channel_id=1, source_target_pairs={{32,0},{40,8},{48,16},{56,24},{0,32},{8,40},{16,48},{24,56},{33,1}... | collective-permute-start | bytes 393224 | tf_op jit(solution)/shard_map/ppermute | solution.py:250
  58.0 0.9 %collective-permute-done.15 = bf16[128,512]{1,0:T(8,128)(2,1)S(1)} collective-permute-done((bf16[128,512]{1,0:T(8,128)(2,1)S(1)}, bf16[128,512]{1,0:T(8,128)(2,1)S(1)}, u32[]{:S(2)}, u32[]{:S(2)}) %collective-permute-start.15) | collective-permute-done | bytes 131104 | tf_op jit(solution)/shard_map/ppermute | solution.py:247
  58.9 3.8 %collective-permute-start.16 = (bf16[128,512]{1,0:T(8,128)(2,1)S(1)}, bf16[128,512]{1,0:T(8,128)(2,1)S(1)}, u32[]{:S(2)}, u32[]{:S(2)}) collective-permute-start(bf16[128,512]{1,0:T(8,128)(2,1)S(1)} %add_convert_fusion.4), channel_id=1, source_target_pairs={{56,0},{0,8},{8,16},{16,24},{24,32},{32,40},{40,48},{48,56},{57,1}... | collective-permute-start | bytes 393224 | tf_op jit(solution)/shard_map/ppermute | solution.py:247
  62.7 3.1 %collective-permute-done.18 = bf16[128,512]{1,0:T(8,128)(2,1)S(1)} collective-permute-done((bf16[128,512]{1,0:T(8,128)(2,1)S(1)}, bf16[128,512]{1,0:T(8,128)(2,1)S(1)}, u32[]{:S(2)}, u32[]{:S(2)}) %collective-permute-start.18) | collective-permute-done | bytes 131104 | tf_op jit(solution)/shard_map/ppermute | solution.py:248
  65.9 3.5 %collective-permute-done.16 = bf16[128,512]{1,0:T(8,128)(2,1)S(1)} collective-permute-done((bf16[128,512]{1,0:T(8,128)(2,1)S(1)}, bf16[128,512]{1,0:T(8,128)(2,1)S(1)}, u32[]{:S(2)}, u32[]{:S(2)}) %collective-permute-start.16) | collective-permute-done | bytes 131104 | tf_op jit(solution)/shard_map/ppermute | solution.py:247
  69.4 3.0 %collective-permute-start.17 = (bf16[128,512]{1,0:T(8,128)(2,1)S(1)}, bf16[128,512]{1,0:T(8,128)(2,1)S(1)}, u32[]{:S(2)}, u32[]{:S(2)}) collective-permute-start(bf16[128,512]{1,0:T(8,128)(2,1)S(1)} %add_convert_fusion.3), channel_id=1, source_target_pairs={{56,0},{0,8},{8,16},{16,24},{24,32},{32,40},{40,48},{48,56},{57,1}... | collective-permute-start | bytes 393224 | tf_op jit(solution)/shard_map/ppermute | solution.py:249
  72.5 2.4 %collective-permute-done.17 = bf16[128,512]{1,0:T(8,128)(2,1)S(1)} collective-permute-done((bf16[128,512]{1,0:T(8,128)(2,1)S(1)}, bf16[128,512]{1,0:T(8,128)(2,1)S(1)}, u32[]{:S(2)}, u32[]{:S(2)}) %collective-permute-start.17) | collective-permute-done | bytes 131104 | tf_op jit(solution)/shard_map/ppermute | solution.py:249
  74.9 3.8 %collective-permute-done.20 = bf16[128,512]{1,0:T(8,128)(2,1)S(1)} collective-permute-done((bf16[128,512]{1,0:T(8,128)(2,1)S(1)}, bf16[128,512]{1,0:T(8,128)(2,1)S(1)}, u32[]{:S(2)}, u32[]{:S(2)}) %collective-permute-start.20) | collective-permute-done | bytes 131104 | tf_op jit(solution)/shard_map/ppermute | solution.py:249
  (36 shorter events, 4.8 us)
Async XLA Ops:
  0.6 1.0 %copy-start = (bf16[128,2048]{1,0:T(8,128)(2,1)S(1)}, bf16[128,2048]{1,0:T(8,128)(2,1)}, u32[]{:S(2)}) copy-start(bf16[128,2048]{1,0:T(8,128)(2,1)} %hidden.1) | copy-start | bytes 1572868
  1.7 7.5 %collective-permute-start = (bf16[128,512]{1,0:T(8,128)(2,1)S(1)}, bf16[128,512]{1,0:T(8,128)(2,1)S(1)}, u32[]{:S(2)}, u32[]{:S(2)}) collective-permute-start(bf16[128,512]{1,0:T(8,128)(2,1)S(1)} %get-tuple-element.31), channel_id=1, source_target_pairs={{0,0},{1,32},{8,8},{9,40},{16,16},{17,48},{24,24},{25,56},{32,1},{... | collective-permute-start | bytes 393224 | tf_op jit(solution)/shard_map/ppermute | solution.py:231
  2.4 6.8 %collective-permute-start.1 = (bf16[128,512]{1,0:T(8,128)(2,1)S(1)}, bf16[128,512]{1,0:T(8,128)(2,1)S(1)}, u32[]{:S(2)}, u32[]{:S(2)}) collective-permute-start(bf16[128,512]{1,0:T(8,128)(2,1)S(1)} %get-tuple-element.32), channel_id=1, source_target_pairs={{0,8},{1,40},{8,16},{9,48},{16,24},{17,56},{24,0},{25,32},{32,9},{... | collective-permute-start | bytes 393224 | tf_op jit(solution)/shard_map/ppermute | solution.py:231
  3.4 11.5 %collective-permute-start.2 = (bf16[128,512]{1,0:T(8,128)(2,1)S(1)}, bf16[128,512]{1,0:T(8,128)(2,1)S(1)}, u32[]{:S(2)}, u32[]{:S(2)}) collective-permute-start(bf16[128,512]{1,0:T(8,128)(2,1)S(1)} %get-tuple-element.33), channel_id=1, source_target_pairs={{0,16},{1,48},{8,24},{9,56},{16,0},{17,32},{24,8},{25,40},{32,17},... | collective-permute-start | bytes 393224 | tf_op jit(solution)/shard_map/ppermute | solution.py:231
  4.0 10.9 %collective-permute-start.3 = (bf16[128,512]{1,0:T(8,128)(2,1)S(1)}, bf16[128,512]{1,0:T(8,128)(2,1)S(1)}, u32[]{:S(2)}, u32[]{:S(2)}) collective-permute-start(bf16[128,512]{1,0:T(8,128)(2,1)S(1)} %get-tuple-element.34), channel_id=1, source_target_pairs={{0,24},{1,56},{8,0},{9,32},{16,8},{17,40},{24,16},{25,48},{32,25},... | collective-permute-start | bytes 393224 | tf_op jit(solution)/shard_map/ppermute | solution.py:231
  14.9 10.4 %collective-permute-start.7 = (bf16[512,512]{1,0:T(8,128)(2,1)S(1)}, bf16[512,512]{1,0:T(8,128)(2,1)S(1)}, u32[]{:S(2)}, u32[]{:S(2)}) collective-permute-start(bf16[512,512]{1,0:T(8,128)(2,1)S(1)} %get-tuple-element.40.refs_8_), channel_id=1, source_target_pairs={{192,0},{0,64},{64,128},{128,192},{193,1},{1,65},{65,129},{129,193... | collective-permute-start | bytes 1572872 | tf_op jit(solution)/shard_map/ppermute | solution.py:238
  15.0 10.4 %collective-permute-start.5 = (bf16[512,512]{1,0:T(8,128)(2,1)S(1)}, bf16[512,512]{1,0:T(8,128)(2,1)S(1)}, u32[]{:S(2)}, u32[]{:S(2)}) collective-permute-start(bf16[512,512]{1,0:T(8,128)(2,1)S(1)} %get-tuple-element.40.refs_8_), channel_id=1, source_target_pairs={{64,0},{128,64},{192,128},{0,192},{65,1},{129,65},{193,129},{1,193... | collective-permute-start | bytes 1572872 | tf_op jit(solution)/shard_map/ppermute | solution.py:238
  18.2 12.3 %collective-permute-start.10 = (bf16[512,512]{1,0:T(8,128)(2,1)S(1)}, bf16[512,512]{1,0:T(8,128)(2,1)S(1)}, u32[]{:S(2)}, u32[]{:S(2)}) collective-permute-start(bf16[512,512]{1,0:T(8,128)(2,1)S(1)} %constant_dynamic-update-slice_fusion.refs_0_), channel_id=1, source_target_pairs={{6,0},{0,2},{2,4},{4,6},{7,1},{1,3},{3,5},{5,7},{14,8},{8,10},{10,... | collective-permute-start | bytes 1572872 | tf_op jit(solution)/shard_map/ppermute | solution.py:237
  18.5 21.2 %collective-permute-start.9 = (bf16[512,512]{1,0:T(8,128)(2,1)S(1)}, bf16[512,512]{1,0:T(8,128)(2,1)S(1)}, u32[]{:S(2)}, u32[]{:S(2)}) collective-permute-start(bf16[512,512]{1,0:T(8,128)(2,1)S(1)} %constant_dynamic-update-slice_fusion.refs_0_), channel_id=1, source_target_pairs={{4,0},{6,2},{0,4},{2,6},{5,1},{7,3},{1,5},{3,7},{12,8},{14,10},{8,... | collective-permute-start | bytes 1572872 | tf_op jit(solution)/shard_map/ppermute | solution.py:237
  21.4 23.9 %collective-permute-start.4 = (bf16[512,512]{1,0:T(8,128)(2,1)S(1)}, bf16[512,512]{1,0:T(8,128)(2,1)S(1)}, u32[]{:S(2)}, u32[]{:S(2)}) collective-permute-start(bf16[512,512]{1,0:T(8,128)(2,1)S(1)} %constant_dynamic-update-slice_fusion.refs_0_), channel_id=1, source_target_pairs={{2,0},{4,2},{6,4},{0,6},{3,1},{5,3},{7,5},{1,7},{10,8},{12,10},{14... | collective-permute-start | bytes 1572872 | tf_op jit(solution)/shard_map/ppermute | solution.py:237
  25.3 20.9 %collective-permute-start.8 = (bf16[256,512]{1,0:T(8,128)(2,1)S(1)}, bf16[256,512]{1,0:T(8,128)(2,1)S(1)}, u32[]{:S(2)}, u32[]{:S(2)}) collective-permute-start(bf16[256,512]{1,0:T(8,128)(2,1)S(1)} %slice.9), channel_id=1, source_target_pairs={{192,0},{0,64},{64,128},{128,192},{193,1},{1,65},{65,129},{129,193... | collective-permute-start | bytes 786440 | tf_op jit(solution)/shard_map/ppermute | solution.py:240
  25.4 20.8 %collective-permute-start.6 = (bf16[256,512]{1,0:T(8,128)(2,1)S(1)}, bf16[256,512]{1,0:T(8,128)(2,1)S(1)}, u32[]{:S(2)}, u32[]{:S(2)}) collective-permute-start(bf16[256,512]{1,0:T(8,128)(2,1)S(1)} %slice.8), channel_id=1, source_target_pairs={{64,0},{128,64},{192,128},{0,192},{65,1},{129,65},{193,129},{1,193... | collective-permute-start | bytes 786440 | tf_op jit(solution)/shard_map/ppermute | solution.py:239
  30.5 15.8 %collective-permute-start.11 = (bf16[512,512]{1,0:T(8,128)(2,1)S(1)}, bf16[512,512]{1,0:T(8,128)(2,1)S(1)}, u32[]{:S(2)}, u32[]{:S(2)}) collective-permute-start(bf16[512,512]{1,0:T(8,128)(2,1)S(1)} %constant_dynamic-update-slice_fusion.refs_0_), channel_id=1, source_target_pairs={{1,0},{0,1},{3,2},{2,3},{5,4},{4,5},{7,6},{6,7},{9,8},{8,9},{11,10... | collective-permute-start | bytes 1572872 | tf_op jit(solution)/shard_map/ppermute | solution.py:243
  39.7 7.1 %collective-permute-start.14 = (bf16[512,512]{1,0:T(8,128)(2,1)S(1)}, bf16[512,512]{1,0:T(8,128)(2,1)S(1)}, u32[]{:S(2)}, u32[]{:S(2)}) collective-permute-start(bf16[512,512]{1,0:T(8,128)(2,1)S(1)} %collective-permute-done.10.refs_3_), channel_id=1, source_target_pairs={{1,0},{0,1},{3,2},{2,3},{5,4},{4,5},{7,6},{6,7},{9,8},{8,9},{11,10... | collective-permute-start | bytes 1572872 | tf_op jit(solution)/shard_map/ppermute | solution.py:243
  45.3 2.4 %collective-permute-start.13 = (bf16[512,512]{1,0:T(8,128)(2,1)S(1)}, bf16[512,512]{1,0:T(8,128)(2,1)S(1)}, u32[]{:S(2)}, u32[]{:S(2)}) collective-permute-start(bf16[512,512]{1,0:T(8,128)(2,1)S(1)} %collective-permute-done.9.refs_2_), channel_id=1, source_target_pairs={{1,0},{0,1},{3,2},{2,3},{5,4},{4,5},{7,6},{6,7},{9,8},{8,9},{11,10... | collective-permute-start | bytes 1572872 | tf_op jit(solution)/shard_map/ppermute | solution.py:243
  46.2 2.3 %collective-permute-start.12 = (bf16[512,512]{1,0:T(8,128)(2,1)S(1)}, bf16[512,512]{1,0:T(8,128)(2,1)S(1)}, u32[]{:S(2)}, u32[]{:S(2)}) collective-permute-start(bf16[512,512]{1,0:T(8,128)(2,1)S(1)} %collective-permute-done.4.refs_1_), channel_id=1, source_target_pairs={{1,0},{0,1},{3,2},{2,3},{5,4},{4,5},{7,6},{6,7},{9,8},{8,9},{11,10... | collective-permute-start | bytes 1572872 | tf_op jit(solution)/shard_map/ppermute | solution.py:243
  51.1 7.8 %collective-permute-start.15 = (bf16[128,512]{1,0:T(8,128)(2,1)S(1)}, bf16[128,512]{1,0:T(8,128)(2,1)S(1)}, u32[]{:S(2)}, u32[]{:S(2)}) collective-permute-start(bf16[128,512]{1,0:T(8,128)(2,1)S(1)} %get-tuple-element.47), channel_id=1, source_target_pairs={{56,0},{0,8},{8,16},{16,24},{24,32},{32,40},{40,48},{48,56},{57,1}... | collective-permute-start | bytes 393224 | tf_op jit(solution)/shard_map/ppermute | solution.py:247
  55.8 9.9 %collective-permute-start.18 = (bf16[128,512]{1,0:T(8,128)(2,1)S(1)}, bf16[128,512]{1,0:T(8,128)(2,1)S(1)}, u32[]{:S(2)}, u32[]{:S(2)}) collective-permute-start(bf16[128,512]{1,0:T(8,128)(2,1)S(1)} %get-tuple-element.50), channel_id=1, source_target_pairs={{8,0},{16,8},{24,16},{32,24},{40,32},{48,40},{56,48},{0,56},{9,1},... | collective-permute-start | bytes 393224 | tf_op jit(solution)/shard_map/ppermute | solution.py:248
  55.8 16.7 %collective-permute-start.21 = (bf16[128,512]{1,0:T(8,128)(2,1)S(1)}, bf16[128,512]{1,0:T(8,128)(2,1)S(1)}, u32[]{:S(2)}, u32[]{:S(2)}) collective-permute-start(bf16[128,512]{1,0:T(8,128)(2,1)S(1)} %get-tuple-element.51), channel_id=1, source_target_pairs={{32,0},{40,8},{48,16},{56,24},{0,32},{8,40},{16,48},{24,56},{33,1}... | collective-permute-start | bytes 393224 | tf_op jit(solution)/shard_map/ppermute | solution.py:250
  58.9 10.4 %collective-permute-start.16 = (bf16[128,512]{1,0:T(8,128)(2,1)S(1)}, bf16[128,512]{1,0:T(8,128)(2,1)S(1)}, u32[]{:S(2)}, u32[]{:S(2)}) collective-permute-start(bf16[128,512]{1,0:T(8,128)(2,1)S(1)} %add_convert_fusion.4), channel_id=1, source_target_pairs={{56,0},{0,8},{8,16},{16,24},{24,32},{32,40},{40,48},{48,56},{57,1}... | collective-permute-start | bytes 393224 | tf_op jit(solution)/shard_map/ppermute | solution.py:247
  65.8 6.6 %collective-permute-start.19 = (bf16[128,512]{1,0:T(8,128)(2,1)S(1)}, bf16[128,512]{1,0:T(8,128)(2,1)S(1)}, u32[]{:S(2)}, u32[]{:S(2)}) collective-permute-start(bf16[128,512]{1,0:T(8,128)(2,1)S(1)} %add_convert_fusion.2), channel_id=1, source_target_pairs={{8,0},{16,8},{24,16},{32,24},{40,32},{48,40},{56,48},{0,56},{9,1},... | collective-permute-start | bytes 393224 | tf_op jit(solution)/shard_map/ppermute | solution.py:248
  69.4 5.5 %collective-permute-start.17 = (bf16[128,512]{1,0:T(8,128)(2,1)S(1)}, bf16[128,512]{1,0:T(8,128)(2,1)S(1)}, u32[]{:S(2)}, u32[]{:S(2)}) collective-permute-start(bf16[128,512]{1,0:T(8,128)(2,1)S(1)} %add_convert_fusion.3), channel_id=1, source_target_pairs={{56,0},{0,8},{8,16},{16,24},{24,32},{32,40},{40,48},{48,56},{57,1}... | collective-permute-start | bytes 393224 | tf_op jit(solution)/shard_map/ppermute | solution.py:249
  72.4 6.3 %collective-permute-start.20 = (bf16[128,512]{1,0:T(8,128)(2,1)S(1)}, bf16[128,512]{1,0:T(8,128)(2,1)S(1)}, u32[]{:S(2)}, u32[]{:S(2)}) collective-permute-start(bf16[128,512]{1,0:T(8,128)(2,1)S(1)} %add_convert_fusion.1), channel_id=1, source_target_pairs={{8,0},{16,8},{24,16},{32,24},{40,32},{48,40},{56,48},{0,56},{9,1},... | collective-permute-start | bytes 393224 | tf_op jit(solution)/shard_map/ppermute | solution.py:249

commit v3 on v2

v3 whole, which is shorter than its diff:
```python
import jax
import jax.numpy as jnp
from jax import lax
from jax.experimental import pallas as pl
from jax.experimental.pallas import tpu as pltpu
from jax.sharding import Mesh, PartitionSpec as P

BLOCK = 512
HALF = 256
ROWS = 128
RIDGE = 0.001
KEEP = 0.75
STEP = 0.003
FLOOR = 1e-06
F32 = jnp.float32
BF16 = jnp.bfloat16
HBM = pl.BlockSpec(memory_space=pltpu.HBM)
VMEM = pl.BlockSpec(memory_space=pltpu.VMEM)


def vmem(one):
    return pltpu.with_memory_space_constraint(one, pltpu.VMEM)


def hbm(one):
    return pltpu.with_memory_space_constraint(one, pltpu.HBM)


def mm(first, second):
    return jnp.dot(first, second, preferred_element_type=F32)


def total(values):
    return jnp.sum(jnp.sum(values, axis=0, keepdims=True), axis=1, keepdims=True)


def unit(size):
    rows = lax.broadcasted_iota(jnp.int32, (size, size), 0)
    cols = lax.broadcasted_iota(jnp.int32, (size, size), 1)
    return rows == cols


def tiles():
    return [(slice(i, i + ROWS), slice(i, i + ROWS)) for i in range(0, BLOCK, ROWS)]


def fresh_roots(statistics, scratch):
    diagonal = unit(ROWS)
    sides = range(len(statistics))
    norms = []
    for statistic in statistics:
        values = statistic[...]
        trace = sum(total(jnp.where(diagonal, statistic[tile], 0.0)) for tile in tiles())
        squares = total(values * values)
        norms.append(jnp.sqrt(squares + 2.0 * RIDGE * trace + BLOCK * RIDGE * RIDGE))
    for i in sides:
        shrink = 0.2 / norms[i]
        scratch[i][...] = statistics[i][...] * shrink
        for tile in tiles():
            scratch[i][tile] += jnp.where(diagonal, RIDGE * shrink, 0.0)
    low = [scratch[i][...].astype(BF16) for i in sides]
    e2 = [mm(low[i], low[i]) for i in sides]
    e3 = [mm(e2[i].astype(BF16), low[i]) for i in sides]
    inner = [(5.0 * e2[i] - 10.0 * scratch[i][...] - e3[i]).astype(BF16) for i in sides]
    tail = [mm(e3[i].astype(BF16), inner[i]) for i in sides]
    a, b = 1.25**2, 1.25**6
    rest = [
        -(a + b) * scratch[i][...] + (5.0 * b) * e2[i] - (10.0 * b) * e3[i] - b * tail[i]
        for i in sides
    ]
    return [one.astype(BF16) for one in rest], [lax.rsqrt(jnp.sqrt(norm)) for norm in norms]


def step_kernel(
    due_hbm, grad_hbm, weight_hbm, sl_hbm, sr_hbm, rl_hbm, rr_hbm,
    nl_hbm, nr_hbm, update_ref, new_ref,
    due_ref, grad_ref, weight_ref, sl, sr, left, right, cond_ref, sems,
):
    copy = pltpu.make_async_copy
    get_grad = copy(grad_hbm, grad_ref, sems.at[0])
    get_sl = copy(sl_hbm, sl, sems.at[1])
    get_sr = copy(sr_hbm, sr, sems.at[2])
    get_weight = copy(weight_hbm, weight_ref, sems.at[3])
    get_rl = copy(rl_hbm, left, sems.at[4])
    get_rr = copy(rr_hbm, right, sems.at[5])
    put_sl = copy(sl, nl_hbm, sems.at[6])
    put_sr = copy(sr, nr_hbm, sems.at[7])
    get_due = copy(due_hbm, due_ref, sems.at[8])
    get_grad.start()
    get_due.start()
    get_sl.start()
    get_sr.start()
    get_weight.start()
    row = lax.axis_index("x") * 8 + lax.axis_index("z")
    col = lax.axis_index("y") * 2 + lax.axis_index("core")
    get_grad.wait()
    get_due.wait()
    due = due_ref[col, row % 16] == row

    @pl.when(jnp.logical_not(due))
    def _():
        get_rl.start()
        get_rr.start()

    grad = grad_ref[...]
    count = 1.0 / (BLOCK * BLOCK)
    grad_norm = jnp.sqrt(total(jnp.square(grad.astype(F32))) * count)
    scale = (1.0 - KEEP) / BLOCK
    gram = lax.dot_general(grad, grad, (((1,), (1,)), ((), ())), preferred_element_type=F32)
    get_sl.wait()
    sl[...] = KEEP * sl[...] + scale * gram
    put_sl.start()
    gram = lax.dot_general(grad, grad, (((0,), (0,)), ((), ())), preferred_element_type=F32)
    get_sr.wait()
    sr[...] = KEEP * sr[...] + scale * gram
    put_sr.start()

    @pl.when(due)
    def _():
        rest, scale = fresh_roots((sl, sr), (left, right))
        half = (1.25**2 * grad.astype(F32) + mm(rest[0], grad)) * scale[0]
        cond_ref[...] = (1.25**2 * half + mm(half.astype(BF16), rest[1])) * scale[1]

    @pl.when(jnp.logical_not(due))
    def _():
        get_rl.wait()
        get_rr.wait()
        on_diagonal = unit(BLOCK)
        used = left[...]
        diag = jnp.sum(jnp.where(on_diagonal, used, 0.0), axis=1, keepdims=True)
        half = diag * grad.astype(F32) + mm(jnp.where(on_diagonal, 0.0, used).astype(BF16), grad)
        used = right[...]
        diag = jnp.sum(jnp.where(on_diagonal, used, 0.0), axis=0, keepdims=True)
        off = jnp.where(on_diagonal, 0.0, used).astype(BF16)
        cond_ref[...] = half * diag + mm(half.astype(BF16), off)

    cond = cond_ref[...]
    graft = grad_norm / jnp.sqrt(total(cond * cond) * count + FLOOR)
    update = (cond * graft).astype(BF16)
    update_ref[...] = update
    get_weight.wait()
    new_ref[...] = (weight_ref[...].astype(F32) - STEP * update.astype(F32)).astype(BF16)
    put_sl.wait()
    put_sr.wait()


def block_step(*operands):
    wide = jax.ShapeDtypeStruct((BLOCK, BLOCK), F32)
    low = jax.ShapeDtypeStruct((BLOCK, BLOCK), BF16)
    return pl.pallas_call(
        step_kernel,
        out_shape=(wide, wide, pltpu.VMEM((BLOCK, BLOCK), BF16), pltpu.VMEM((BLOCK, BLOCK), BF16)),
        in_specs=[HBM] * 7,
        out_specs=(HBM, HBM, VMEM, VMEM),
        scratch_shapes=[pltpu.SMEM((8, 16), jnp.int32)]
        + [pltpu.VMEM((BLOCK, BLOCK), BF16) for _ in range(2)]
        + [pltpu.VMEM((BLOCK, BLOCK), F32) for _ in range(5)]
        + [pltpu.SemaphoreType.DMA((9,))],
        compiler_params=pltpu.CompilerParams(vmem_limit_bytes=24 * 1024 * 1024),
        cost_estimate=pl.CostEstimate(
            flops=2 * 30 * BLOCK**3, bytes_accessed=9 * 1024 * 1024, transcendentals=0
        ),
        name="block_step",
    )(*[hbm(one) for one in operands])


def split_kernel(hidden, *outs):
    place = lax.axis_index("z") % 4
    for shift in range(4):
        start = pl.multiple_of(((place + shift) % 4) * BLOCK, BLOCK)
        outs[shift][...] = hidden[:, pl.ds(start, BLOCK)]


def split_hidden(hidden):
    part = pltpu.VMEM((ROWS, BLOCK), BF16)
    return pl.pallas_call(
        split_kernel,
        out_shape=(part,) * 4,
        in_specs=[VMEM],
        out_specs=(VMEM,) * 4,
        compiler_params=pltpu.CompilerParams(vmem_limit_bytes=4 * 1024 * 1024),
        cost_estimate=pl.CostEstimate(flops=0, bytes_accessed=1024 * 1024, transcendentals=0),
        name="split_hidden",
    )(hidden)


def multiply(acc, blocks, placed):
    y = lax.axis_index("y")
    for j in range(1, 4):
        acc += mm(blocks[j - 1][...], placed[(y + j) % 4])
    return acc


def near_kernel(*refs):
    near, far, weights = refs[0:4], refs[4], refs[5:10]
    near_sum, far_sum, placed, sems = refs[10:14]
    x, y = lax.axis_index("x"), lax.axis_index("y")
    opposite = placed.at[(x + 2) % 4]
    homes = [
        placed.at[x],
        placed.at[(x + 1) % 4],
        opposite.at[pl.ds(0, HALF)],
        opposite.at[pl.ds(HALF, HALF)],
        placed.at[(x + 3) % 4],
    ]
    copies = [pltpu.make_async_copy(weights[i], homes[i], sems.at[i]) for i in range(5)]
    for one in copies:
        one.start()
    for one in copies:
        one.wait()
    near_sum[...] = multiply(mm(near[0][...], placed[y]), near[1:], placed)
    far_sum[...] = mm(far[...], placed[y])


def project_near(near, far, weights):
    wide = pltpu.VMEM((BLOCK, BLOCK), F32)
    return pl.pallas_call(
        near_kernel,
        out_shape=(wide, wide, pltpu.VMEM((4, BLOCK, BLOCK), BF16)),
        in_specs=[VMEM] * 10,
        out_specs=(VMEM,) * 3,
        scratch_shapes=[pltpu.SemaphoreType.DMA((5,))],
        compiler_params=pltpu.CompilerParams(vmem_limit_bytes=16 * 1024 * 1024),
        cost_estimate=pl.CostEstimate(
            flops=2 * 512 * 2048 * BLOCK, bytes_accessed=7 * 1024 * 1024, transcendentals=0
        ),
        name="project_near",
    )(*[vmem(one) for one in (*near, far, *weights)])


def far_kernel(*refs):
    far, near_sum, far_part, placed, outs = refs[0:3], refs[3], refs[4], refs[5], refs[6:14]
    z, core = lax.axis_index("z"), lax.axis_index("core")
    far_sum = multiply(far_part[...], far, placed)
    for s in range(8):
        piece = -s % 4
        rows = slice(piece * ROWS, (piece + 1) * ROWS)
        is_near = ((z + s) % 8) // 4 == core
        outs[s][...] = jnp.where(is_near, near_sum[rows], far_sum[rows]).astype(outs[s].dtype)


def project_far(far, near_sum, far_part, placed):
    part = pltpu.VMEM((ROWS, BLOCK), BF16)
    return pl.pallas_call(
        far_kernel,
        out_shape=(pltpu.VMEM((ROWS, BLOCK), F32),) + (part,) * 7,
        in_specs=[VMEM] * 6,
        out_specs=(VMEM,) * 8,
        compiler_params=pltpu.CompilerParams(vmem_limit_bytes=16 * 1024 * 1024),
        cost_estimate=pl.CostEstimate(
            flops=2 * 512 * 2048 * BLOCK, bytes_accessed=7 * 1024 * 1024, transcendentals=0
        ),
        name="project_far",
    )(*[vmem(one) for one in (*far, near_sum, far_part, placed)])


def ring(size, shift):
    return [((i + shift) % size, i) for i in range(size)]


def add(first, second):
    return (first.astype(F32) + second.astype(F32)).astype(BF16)


def body(hidden, weight, gradient, stats_left, stats_right, root_left, root_right, due_rows):
    pieces = split_hidden(hidden)
    tokens = []
    for shift in range(4):
        perm = []
        for z in range(8):
            for core in range(2):
                perm.append((z * 2 + core, (core * 4 + (z % 4 + shift) % 4) * 2 + z // 4))
        tokens.append(lax.ppermute(pieces[shift], ("z", "core"), perm))
    new_left, new_right, update, new_weight = block_step(
        due_rows.T, gradient, weight, stats_left, stats_right, root_left, root_right
    )
    *tokens, _ = lax.optimization_barrier((*tokens, new_weight))
    own = jnp.concatenate(tokens, axis=0)
    near = [own] + [lax.ppermute(own, "y", ring(4, j)) for j in (1, 2, 3)]
    one, three = (lax.ppermute(new_weight, "x", ring(4, i)) for i in (1, 3))
    top = lax.ppermute(one[:HALF], "x", ring(4, 1))
    bottom = lax.ppermute(three[HALF:], "x", ring(4, 3))
    near[1], top, bottom = lax.optimization_barrier((near[1], top, bottom))
    weights = [new_weight, one, top, bottom, three]
    far = [lax.ppermute(piece, "core", ring(2, 1)) for piece in near]
    parts = project_far(far[1:], *project_near(near, far[0], weights))
    up, down = parts[3], parts[5]
    for near_up, near_down in ((parts[2], parts[6]), (parts[1], parts[7])):
        up = add(near_up, lax.ppermute(up, "z", ring(8, 7)))
        down = add(near_down, lax.ppermute(down, "z", ring(8, 1)))
    up, down = lax.ppermute(up, "z", ring(8, 7)), lax.ppermute(down, "z", ring(8, 1))
    far_sum = lax.ppermute(parts[4], "z", ring(8, 4))
    projected = parts[0] + up.astype(F32) + down.astype(F32) + far_sum.astype(F32)
    return (new_left, new_right, update, projected.astype(BF16))


def solution(mesh):
    grid = Mesh(mesh.devices.reshape(4, 8, 4, 2), ("x", "z", "y", "core"))
    spec = P(("x", "z"), ("y", "core"))
    return jax.shard_map(
        body,
        mesh=grid,
        in_specs=(spec,) * 7 + (P(),),
        out_specs=(spec,) * 4,
        check_vma=False,
    )
```

time: 79.5 us -> 76.3 us (0.960)
  waiting for transfers between devices: 25.8 us -> 17.7 us
  starting transfers between devices: 43.6 us -> 48 us
  local copies, waits for them, and re-layouts: 1.11 us -> 1.91 us
    ppermute x4, waiting for transfers between devices: 5.65 us -> 1.59 us  [body(): tokens.append(lax.ppermute(pieces[shift], ('z', 'core'), perm))]
    ppermute x4, starting transfers between devices: 15.8 us -> 18.8 us  [body(): far = [lax.ppermute(piece, 'core', ring(2, 1)) for piece in near]]
    ppermute x4, waiting for transfers between devices: 2.19 us -> 0.45 us  [body(): far = [lax.ppermute(piece, 'core', ring(2, 1)) for piece in near]]
    ppermute x2, starting transfers between devices: 3.24 us -> 4.69 us  [body(): one, three = (lax.ppermute(new_weight, 'x', ring(4, i)) for i in (1, 3))]
    ppermute x3, starting transfers between devices: 4.54 us -> 3.33 us  [body(): near = [own] + [lax.ppermute(own, 'y', ring(4, j)) for j in (1, 2, 3)]]
    ppermute x2, waiting for transfers between devices: 2.54 us -> 1.7 us  [body(): one, three = (lax.ppermute(new_weight, 'x', ring(4, i)) for i in (1, 3))]
    unnamed x5 -> x6, local copies, waits for them, and re-layouts: 1.07 us -> 1.86 us
    pallas_call x2 -> x3, Pallas kernels: 7.24 us -> 6.81 us  [the longest x1 4.11 us: block_step(): pl.pallas_call(step_kernel, out_shape=(wide, wide, pltpu.VMEM((BLOCK, BLO...]
  transfers between devices with their start and end apart: 22 -> 22, of which waited for: 11 -> 10; matrix products, arithmetic and copies ran while one was open for 0% -> 1% of each run, Pallas kernels for 6% -> 8%
where the time goes in v3:
time: 76.3 us; the launch traced here: 76.2 us
  starting transfers between devices  48 us (63%)
  waiting for transfers between devices  17.7 us (23%)
  Pallas kernels  6.85 us (9%)
  local copies, waits for them, and re-layouts  1.91 us (3%)
  other arithmetic  0.85 us (1%)
  between operations  0.79 us (1%)
    ppermute x4, starting transfers between devices, body(): far = [lax.ppermute(piece, 'core', ring(2, 1)) for piece in near]  18.8 us
    ppermute x2, starting transfers between devices, body(): up = add(near_up, lax.ppermute(up, 'z', ring(8, 7)))  9.05 us
    ppermute x2, starting transfers between devices, body(): one, three = (lax.ppermute(new_weight, 'x', ring(4, i)) for i in (1, 3))  4.69 us
    ppermute x2, waiting for transfers between devices, body(): up = add(near_up, lax.ppermute(up, 'z', ring(8, 7)))  4.31 us
    pallas_call x1, Pallas kernels, block_step(): pl.pallas_call(step_kernel, out_shape=(wide, wide, pltpu.VMEM((BLOCK, BLO...  4.11 us
    ppermute x1, waiting for transfers between devices, body(): lax.ppermute(down, 'z', ring(8, 1))  3.77 us
    ppermute x1, starting transfers between devices, body(): top = lax.ppermute(one[:HALF], 'x', ring(4, 1))  3.77 us
    ppermute x3, starting transfers between devices, body(): near = [own] + [lax.ppermute(own, 'y', ring(4, j)) for j in (1, 2, 3)]  3.33 us
  transfers between devices with their start and end apart: 22, of which 10 were waited for; matrix products, arithmetic and copies ran while one was open for 1% of the time, Pallas kernels for 8%

profile of v3, /device:TPU:96, one launch (start us, length us, event | category | flops | bytes accessed | tf_op | source)
XLA Modules:
  0.0 76.2 jit_solution(17168138973735479248)
XLA Ops:
  0.6 1.0 %copy-done = bf16[128,2048]{1,0:T(8,128)(2,1)S(1)} copy-done((bf16[128,2048]{1,0:T(8,128)(2,1)S(1)}, bf16[128,2048]{1,0:T(8,128)(2,1)}, u32[]{:S(2)}) %copy-start) | copy-done | bytes 524312
  2.4 1.0 %collective-permute-start.1 = (bf16[128,512]{1,0:T(8,128)(2,1)S(1)}, bf16[128,512]{1,0:T(8,128)(2,1)S(1)}, u32[]{:S(2)}, u32[]{:S(2)}) collective-permute-start(bf16[128,512]{1,0:T(8,128)(2,1)S(1)} %get-tuple-element.34), channel_id=1, source_target_pairs={{0,8},{1,40},{8,16},{9,48},{16,24},{17,56},{24,0},{25,32},{32,9},{... | collective-permute-start | bytes 393224 | tf_op jit(solution)/shard_map/ppermute | solution.py:273
  4.5 4.1 %block_step.1 = (f32[512,512]{1,0:T(8,128)}, f32[512,512]{1,0:T(8,128)}, bf16[512,512]{1,0:T(8,128)(2,1)S(1)}, bf16[512,512]{1,0:T(8,128)(2,1)S(1)}) custom-call(s32[8,16]{1,0:T(8,128)} %bitcast.1, bf16[512,512]{1,0:T(8,128)(2,1)} %grad_hbm.1, bf16[512,512]{1,0:T(8,128)(2,1)} %weight_hbm.1, f32[512,512]{1,0:T(8,128)} %sl_hbm.1, f32[512,512]{1,0:T(8,128)} %sr_hbm.1, ...), custom_call_target="tpu_custom_call" | custom-call | flops 8053063680 | bytes 9437184 | tf_op jit(solution)/shard_map/block_step/pallas_call | solution.py:150
  8.6 4.7 %collective-permute-start.5 = (bf16[512,512]{1,0:T(8,128)(2,1)S(1)}, bf16[512,512]{1,0:T(8,128)(2,1)S(1)}, u32[]{:S(2)}, u32[]{:S(2)}) collective-permute-start(bf16[512,512]{1,0:T(8,128)(2,1)S(1)} %get-tuple-element.37.refs_5_), channel_id=1, source_target_pairs={{64,0},{128,64},{192,128},{0,192},{65,1},{129,65},{193,129},{1,193... | collective-permute-start | bytes 1572872 | tf_op jit(solution)/shard_map/ppermute | solution.py:280
  13.3 1.6 %collective-permute-done.2 = bf16[128,512]{1,0:T(8,128)(2,1)S(1)} collective-permute-done((bf16[128,512]{1,0:T(8,128)(2,1)S(1)}, bf16[128,512]{1,0:T(8,128)(2,1)S(1)}, u32[]{:S(2)}, u32[]{:S(2)}) %collective-permute-start.2) | collective-permute-done | bytes 131104 | tf_op jit(solution)/shard_map/ppermute | solution.py:273
  15.0 1.7 %collective-permute-start.4 = (bf16[512,512]{1,0:T(8,128)(2,1)S(1)}, bf16[512,512]{1,0:T(8,128)(2,1)S(1)}, u32[]{:S(2)}, u32[]{:S(2)}) collective-permute-start(bf16[512,512]{1,0:T(8,128)(2,1)S(1)} %constant_dynamic-update-slice_fusion.refs_0_), channel_id=1, source_target_pairs={{2,0},{4,2},{6,4},{0,6},{3,1},{5,3},{7,5},{1,7},{10,8},{12,10},{14... | collective-permute-start | bytes 1572872 | tf_op jit(solution)/shard_map/ppermute | solution.py:279
  17.3 1.0 %collective-permute-start.12 = (bf16[512,512]{1,0:T(8,128)(2,1)S(1)}, bf16[512,512]{1,0:T(8,128)(2,1)S(1)}, u32[]{:S(2)}, u32[]{:S(2)}) collective-permute-start(bf16[512,512]{1,0:T(8,128)(2,1)S(1)} %constant_dynamic-update-slice_fusion.refs_0_), channel_id=1, source_target_pairs={{6,0},{0,2},{2,4},{4,6},{7,1},{1,3},{3,5},{5,7},{14,8},{8,10},{10,... | collective-permute-start | bytes 1572872 | tf_op jit(solution)/shard_map/ppermute | solution.py:279
  18.3 1.7 %collective-permute-done.5.refs_6_ = bf16[512,512]{1,0:T(8,128)(2,1)S(1)} collective-permute-done((bf16[512,512]{1,0:T(8,128)(2,1)S(1)}, bf16[512,512]{1,0:T(8,128)(2,1)S(1)}, u32[]{:S(2)}, u32[]{:S(2)}) %collective-permute-start.5) | collective-permute-done | bytes 524320 | tf_op jit(solution)/shard_map/ppermute | solution.py:280
  20.0 3.8 %collective-permute-start.6 = (bf16[256,512]{1,0:T(8,128)(2,1)S(1)}, bf16[256,512]{1,0:T(8,128)(2,1)S(1)}, u32[]{:S(2)}, u32[]{:S(2)}) collective-permute-start(bf16[256,512]{1,0:T(8,128)(2,1)S(1)} %slice.8), channel_id=1, source_target_pairs={{64,0},{128,64},{192,128},{0,192},{65,1},{129,65},{193,129},{1,193... | collective-permute-start | bytes 786440 | tf_op jit(solution)/shard_map/ppermute | solution.py:281
  24.2 16.7 %collective-permute-start.14 = (bf16[512,512]{1,0:T(8,128)(2,1)S(1)}, bf16[512,512]{1,0:T(8,128)(2,1)S(1)}, u32[]{:S(2)}, u32[]{:S(2)}) collective-permute-start(bf16[512,512]{1,0:T(8,128)(2,1)S(1)} %constant_dynamic-update-slice_fusion.refs_0_), channel_id=1, source_target_pairs={{1,0},{0,1},{3,2},{2,3},{5,4},{4,5},{7,6},{6,7},{9,8},{8,9},{11,10... | collective-permute-start | bytes 1572872 | tf_op jit(solution)/shard_map/ppermute | solution.py:285
  41.0 1.1 %collective-permute-done.12.refs_3_ = bf16[512,512]{1,0:T(8,128)(2,1)S(1)} collective-permute-done((bf16[512,512]{1,0:T(8,128)(2,1)S(1)}, bf16[512,512]{1,0:T(8,128)(2,1)S(1)}, u32[]{:S(2)}, u32[]{:S(2)}) %collective-permute-start.12) | collective-permute-done | bytes 524320 | tf_op jit(solution)/shard_map/ppermute | solution.py:279
  42.0 2.0 %collective-permute-start.13 = (bf16[512,512]{1,0:T(8,128)(2,1)S(1)}, bf16[512,512]{1,0:T(8,128)(2,1)S(1)}, u32[]{:S(2)}, u32[]{:S(2)}) collective-permute-start(bf16[512,512]{1,0:T(8,128)(2,1)S(1)} %collective-permute-done.12.refs_3_), channel_id=1, source_target_pairs={{1,0},{0,1},{3,2},{2,3},{5,4},{4,5},{7,6},{6,7},{9,8},{8,9},{11,10... | collective-permute-start | bytes 1572872 | tf_op jit(solution)/shard_map/ppermute | solution.py:285
  44.2 1.7 %project_near.1 = (f32[512,512]{1,0:T(8,128)S(1)}, f32[512,512]{1,0:T(8,128)S(1)}, bf16[4,512,512]{2,1,0:T(8,128)(2,1)S(1)}) custom-call(bf16[512,512]{1,0:T(8,128)(2,1)S(1)} %constant_dynamic-update-slice_fusion.refs_0_, bf16[512,512]{1,0:T(8,128)(2,1)S(1)} %collective-permute-done.4.refs_1_, bf16[512,512]{1,0:T(8,128)(2,1)S(1)} %collective-permute-done.10.refs_2_, ...), custom_call_target="tpu_custom_call" | custom-call | flops 1073741824 | bytes 7340032 | tf_op jit(solution)/shard_map/project_near/pallas_call | solution.py:217
  46.3 1.0 %project_far.1 = (f32[128,512]{1,0:T(8,128)S(1)}, bf16[128,512]{1,0:T(8,128)(2,1)S(1)}, bf16[128,512]{1,0:T(8,128)(2,1)S(1)}, bf16[128,512]{1,0:T(8,128)(2,1)S(1...) custom-call(bf16[512,512]{1,0:T(8,128)(2,1)S(1)} %collective-permute, ...), custom_call_target="tpu_custom_call" | custom-call | flops 1073741824 | bytes 7340032 | tf_op jit(solution)/shard_map/project_far/pallas_call | solution.py:244
  47.3 5.3 %collective-permute-start.15 = (bf16[128,512]{1,0:T(8,128)(2,1)S(1)}, bf16[128,512]{1,0:T(8,128)(2,1)S(1)}, u32[]{:S(2)}, u32[]{:S(2)}) collective-permute-start(bf16[128,512]{1,0:T(8,128)(2,1)S(1)} %get-tuple-element.51), channel_id=1, source_target_pairs={{56,0},{0,8},{8,16},{16,24},{24,32},{32,40},{40,48},{48,56},{57,1}... | collective-permute-start | bytes 393224 | tf_op jit(solution)/shard_map/ppermute | solution.py:289
  52.6 2.2 %collective-permute-start.21 = (bf16[128,512]{1,0:T(8,128)(2,1)S(1)}, bf16[128,512]{1,0:T(8,128)(2,1)S(1)}, u32[]{:S(2)}, u32[]{:S(2)}) collective-permute-start(bf16[128,512]{1,0:T(8,128)(2,1)S(1)} %get-tuple-element.55), channel_id=1, source_target_pairs={{32,0},{40,8},{48,16},{56,24},{0,32},{8,40},{16,48},{24,56},{33,1}... | collective-permute-start | bytes 393224 | tf_op jit(solution)/shard_map/ppermute | solution.py:292
  54.8 0.9 %collective-permute-done.15 = bf16[128,512]{1,0:T(8,128)(2,1)S(1)} collective-permute-done((bf16[128,512]{1,0:T(8,128)(2,1)S(1)}, bf16[128,512]{1,0:T(8,128)(2,1)S(1)}, u32[]{:S(2)}, u32[]{:S(2)}) %collective-permute-start.15) | collective-permute-done | bytes 131104 | tf_op jit(solution)/shard_map/ppermute | solution.py:289
  55.7 3.8 %collective-permute-start.16 = (bf16[128,512]{1,0:T(8,128)(2,1)S(1)}, bf16[128,512]{1,0:T(8,128)(2,1)S(1)}, u32[]{:S(2)}, u32[]{:S(2)}) collective-permute-start(bf16[128,512]{1,0:T(8,128)(2,1)S(1)} %add_convert_fusion.4), channel_id=1, source_target_pairs={{56,0},{0,8},{8,16},{16,24},{24,32},{32,40},{40,48},{48,56},{57,1}... | collective-permute-start | bytes 393224 | tf_op jit(solution)/shard_map/ppermute | solution.py:289
  59.5 3.1 %collective-permute-done.18 = bf16[128,512]{1,0:T(8,128)(2,1)S(1)} collective-permute-done((bf16[128,512]{1,0:T(8,128)(2,1)S(1)}, bf16[128,512]{1,0:T(8,128)(2,1)S(1)}, u32[]{:S(2)}, u32[]{:S(2)}) %collective-permute-start.18) | collective-permute-done | bytes 131104 | tf_op jit(solution)/shard_map/ppermute | solution.py:290
  62.7 3.5 %collective-permute-done.16 = bf16[128,512]{1,0:T(8,128)(2,1)S(1)} collective-permute-done((bf16[128,512]{1,0:T(8,128)(2,1)S(1)}, bf16[128,512]{1,0:T(8,128)(2,1)S(1)}, u32[]{:S(2)}, u32[]{:S(2)}) %collective-permute-start.16) | collective-permute-done | bytes 131104 | tf_op jit(solution)/shard_map/ppermute | solution.py:289
  66.2 3.0 %collective-permute-start.17 = (bf16[128,512]{1,0:T(8,128)(2,1)S(1)}, bf16[128,512]{1,0:T(8,128)(2,1)S(1)}, u32[]{:S(2)}, u32[]{:S(2)}) collective-permute-start(bf16[128,512]{1,0:T(8,128)(2,1)S(1)} %add_convert_fusion.3), channel_id=1, source_target_pairs={{56,0},{0,8},{8,16},{16,24},{24,32},{32,40},{40,48},{48,56},{57,1}... | collective-permute-start | bytes 393224 | tf_op jit(solution)/shard_map/ppermute | solution.py:291
  69.3 0.8 %copy.15 = bf16[512,512]{1,0:T(8,128)(2,1)} copy(bf16[512,512]{1,0:T(8,128)(2,1)S(1)} %get-tuple-element.58) | data formatting | bytes 1048576
  70.1 1.6 %collective-permute-done.17 = bf16[128,512]{1,0:T(8,128)(2,1)S(1)} collective-permute-done((bf16[128,512]{1,0:T(8,128)(2,1)S(1)}, bf16[128,512]{1,0:T(8,128)(2,1)S(1)}, u32[]{:S(2)}, u32[]{:S(2)}) %collective-permute-start.17) | collective-permute-done | bytes 131104 | tf_op jit(solution)/shard_map/ppermute | solution.py:291
  71.7 3.8 %collective-permute-done.20 = bf16[128,512]{1,0:T(8,128)(2,1)S(1)} collective-permute-done((bf16[128,512]{1,0:T(8,128)(2,1)S(1)}, bf16[128,512]{1,0:T(8,128)(2,1)S(1)}, u32[]{:S(2)}, u32[]{:S(2)}) %collective-permute-start.20) | collective-permute-done | bytes 131104 | tf_op jit(solution)/shard_map/ppermute | solution.py:291
  (38 shorter events, 4.5 us)
Async XLA Ops:
  0.6 1.0 %copy-start = (bf16[128,2048]{1,0:T(8,128)(2,1)S(1)}, bf16[128,2048]{1,0:T(8,128)(2,1)}, u32[]{:S(2)}) copy-start(bf16[128,2048]{1,0:T(8,128)(2,1)} %hidden.1) | copy-start | bytes 1572868
  1.7 11.6 %collective-permute-start = (bf16[128,512]{1,0:T(8,128)(2,1)S(1)}, bf16[128,512]{1,0:T(8,128)(2,1)S(1)}, u32[]{:S(2)}, u32[]{:S(2)}) collective-permute-start(bf16[128,512]{1,0:T(8,128)(2,1)S(1)} %get-tuple-element.33), channel_id=1, source_target_pairs={{0,0},{1,32},{8,8},{9,40},{16,16},{17,48},{24,24},{25,56},{32,1},{... | collective-permute-start | bytes 393224 | tf_op jit(solution)/shard_map/ppermute | solution.py:273
  2.4 10.9 %collective-permute-start.1 = (bf16[128,512]{1,0:T(8,128)(2,1)S(1)}, bf16[128,512]{1,0:T(8,128)(2,1)S(1)}, u32[]{:S(2)}, u32[]{:S(2)}) collective-permute-start(bf16[128,512]{1,0:T(8,128)(2,1)S(1)} %get-tuple-element.34), channel_id=1, source_target_pairs={{0,8},{1,40},{8,16},{9,48},{16,24},{17,56},{24,0},{25,32},{32,9},{... | collective-permute-start | bytes 393224 | tf_op jit(solution)/shard_map/ppermute | solution.py:273
  3.4 11.5 %collective-permute-start.2 = (bf16[128,512]{1,0:T(8,128)(2,1)S(1)}, bf16[128,512]{1,0:T(8,128)(2,1)S(1)}, u32[]{:S(2)}, u32[]{:S(2)}) collective-permute-start(bf16[128,512]{1,0:T(8,128)(2,1)S(1)} %get-tuple-element.35), channel_id=1, source_target_pairs={{0,16},{1,48},{8,24},{9,56},{16,0},{17,32},{24,8},{25,40},{32,17},... | collective-permute-start | bytes 393224 | tf_op jit(solution)/shard_map/ppermute | solution.py:273
  4.0 10.9 %collective-permute-start.3 = (bf16[128,512]{1,0:T(8,128)(2,1)S(1)}, bf16[128,512]{1,0:T(8,128)(2,1)S(1)}, u32[]{:S(2)}, u32[]{:S(2)}) collective-permute-start(bf16[128,512]{1,0:T(8,128)(2,1)S(1)} %get-tuple-element.36), channel_id=1, source_target_pairs={{0,24},{1,56},{8,0},{9,32},{16,8},{17,40},{24,16},{25,48},{32,25},... | collective-permute-start | bytes 393224 | tf_op jit(solution)/shard_map/ppermute | solution.py:273
  8.6 11.4 %collective-permute-start.5 = (bf16[512,512]{1,0:T(8,128)(2,1)S(1)}, bf16[512,512]{1,0:T(8,128)(2,1)S(1)}, u32[]{:S(2)}, u32[]{:S(2)}) collective-permute-start(bf16[512,512]{1,0:T(8,128)(2,1)S(1)} %get-tuple-element.37.refs_5_), channel_id=1, source_target_pairs={{64,0},{128,64},{192,128},{0,192},{65,1},{129,65},{193,129},{1,193... | collective-permute-start | bytes 1572872 | tf_op jit(solution)/shard_map/ppermute | solution.py:280
  13.3 10.5 %collective-permute-start.7 = (bf16[512,512]{1,0:T(8,128)(2,1)S(1)}, bf16[512,512]{1,0:T(8,128)(2,1)S(1)}, u32[]{:S(2)}, u32[]{:S(2)}) collective-permute-start(bf16[512,512]{1,0:T(8,128)(2,1)S(1)} %get-tuple-element.37.refs_5_), channel_id=1, source_target_pairs={{192,0},{0,64},{64,128},{128,192},{193,1},{1,65},{65,129},{129,193... | collective-permute-start | bytes 1572872 | tf_op jit(solution)/shard_map/ppermute | solution.py:280
  15.0 9.3 %collective-permute-start.4 = (bf16[512,512]{1,0:T(8,128)(2,1)S(1)}, bf16[512,512]{1,0:T(8,128)(2,1)S(1)}, u32[]{:S(2)}, u32[]{:S(2)}) collective-permute-start(bf16[512,512]{1,0:T(8,128)(2,1)S(1)} %constant_dynamic-update-slice_fusion.refs_0_), channel_id=1, source_target_pairs={{2,0},{4,2},{6,4},{0,6},{3,1},{5,3},{7,5},{1,7},{10,8},{12,10},{14... | collective-permute-start | bytes 1572872 | tf_op jit(solution)/shard_map/ppermute | solution.py:279
  16.7 24.3 %collective-permute-start.10 = (bf16[512,512]{1,0:T(8,128)(2,1)S(1)}, bf16[512,512]{1,0:T(8,128)(2,1)S(1)}, u32[]{:S(2)}, u32[]{:S(2)}) collective-permute-start(bf16[512,512]{1,0:T(8,128)(2,1)S(1)} %constant_dynamic-update-slice_fusion.refs_0_), channel_id=1, source_target_pairs={{4,0},{6,2},{0,4},{2,6},{5,1},{7,3},{1,5},{3,7},{12,8},{14,10},{8,... | collective-permute-start | bytes 1572872 | tf_op jit(solution)/shard_map/ppermute | solution.py:279
  17.3 24.7 %collective-permute-start.12 = (bf16[512,512]{1,0:T(8,128)(2,1)S(1)}, bf16[512,512]{1,0:T(8,128)(2,1)S(1)}, u32[]{:S(2)}, u32[]{:S(2)}) collective-permute-start(bf16[512,512]{1,0:T(8,128)(2,1)S(1)} %constant_dynamic-update-slice_fusion.refs_0_), channel_id=1, source_target_pairs={{6,0},{0,2},{2,4},{4,6},{7,1},{1,3},{3,5},{5,7},{14,8},{8,10},{10,... | collective-permute-start | bytes 1572872 | tf_op jit(solution)/shard_map/ppermute | solution.py:279
  20.0 24.0 %collective-permute-start.6 = (bf16[256,512]{1,0:T(8,128)(2,1)S(1)}, bf16[256,512]{1,0:T(8,128)(2,1)S(1)}, u32[]{:S(2)}, u32[]{:S(2)}) collective-permute-start(bf16[256,512]{1,0:T(8,128)(2,1)S(1)} %slice.8), channel_id=1, source_target_pairs={{64,0},{128,64},{192,128},{0,192},{65,1},{129,65},{193,129},{1,193... | collective-permute-start | bytes 786440 | tf_op jit(solution)/shard_map/ppermute | solution.py:281
  23.8 20.3 %collective-permute-start.8 = (bf16[256,512]{1,0:T(8,128)(2,1)S(1)}, bf16[256,512]{1,0:T(8,128)(2,1)S(1)}, u32[]{:S(2)}, u32[]{:S(2)}) collective-permute-start(bf16[256,512]{1,0:T(8,128)(2,1)S(1)} %slice.9), channel_id=1, source_target_pairs={{192,0},{0,64},{64,128},{128,192},{193,1},{1,65},{65,129},{129,193... | collective-permute-start | bytes 786440 | tf_op jit(solution)/shard_map/ppermute | solution.py:282
  24.2 19.9 %collective-permute-start.14 = (bf16[512,512]{1,0:T(8,128)(2,1)S(1)}, bf16[512,512]{1,0:T(8,128)(2,1)S(1)}, u32[]{:S(2)}, u32[]{:S(2)}) collective-permute-start(bf16[512,512]{1,0:T(8,128)(2,1)S(1)} %constant_dynamic-update-slice_fusion.refs_0_), channel_id=1, source_target_pairs={{1,0},{0,1},{3,2},{2,3},{5,4},{4,5},{7,6},{6,7},{9,8},{8,9},{11,10... | collective-permute-start | bytes 1572872 | tf_op jit(solution)/shard_map/ppermute | solution.py:285
  40.9 4.9 %collective-permute-start.11 = (bf16[512,512]{1,0:T(8,128)(2,1)S(1)}, bf16[512,512]{1,0:T(8,128)(2,1)S(1)}, u32[]{:S(2)}, u32[]{:S(2)}) collective-permute-start(bf16[512,512]{1,0:T(8,128)(2,1)S(1)} %collective-permute-done.10.refs_2_), channel_id=1, source_target_pairs={{1,0},{0,1},{3,2},{2,3},{5,4},{4,5},{7,6},{6,7},{9,8},{8,9},{11,10... | collective-permute-start | bytes 1572872 | tf_op jit(solution)/shard_map/ppermute | solution.py:285
  42.0 3.8 %collective-permute-start.13 = (bf16[512,512]{1,0:T(8,128)(2,1)S(1)}, bf16[512,512]{1,0:T(8,128)(2,1)S(1)}, u32[]{:S(2)}, u32[]{:S(2)}) collective-permute-start(bf16[512,512]{1,0:T(8,128)(2,1)S(1)} %collective-permute-done.12.refs_3_), channel_id=1, source_target_pairs={{1,0},{0,1},{3,2},{2,3},{5,4},{4,5},{7,6},{6,7},{9,8},{8,9},{11,10... | collective-permute-start | bytes 1572872 | tf_op jit(solution)/shard_map/ppermute | solution.py:285
  44.1 2.3 %collective-permute-start.9 = (bf16[512,512]{1,0:T(8,128)(2,1)S(1)}, bf16[512,512]{1,0:T(8,128)(2,1)S(1)}, u32[]{:S(2)}, u32[]{:S(2)}) collective-permute-start(bf16[512,512]{1,0:T(8,128)(2,1)S(1)} %collective-permute-done.4.refs_1_), channel_id=1, source_target_pairs={{1,0},{0,1},{3,2},{2,3},{5,4},{4,5},{7,6},{6,7},{9,8},{8,9},{11,10... | collective-permute-start | bytes 1572872 | tf_op jit(solution)/shard_map/ppermute | solution.py:285
  47.3 8.3 %collective-permute-start.15 = (bf16[128,512]{1,0:T(8,128)(2,1)S(1)}, bf16[128,512]{1,0:T(8,128)(2,1)S(1)}, u32[]{:S(2)}, u32[]{:S(2)}) collective-permute-start(bf16[128,512]{1,0:T(8,128)(2,1)S(1)} %get-tuple-element.51), channel_id=1, source_target_pairs={{56,0},{0,8},{8,16},{16,24},{24,32},{32,40},{40,48},{48,56},{57,1}... | collective-permute-start | bytes 393224 | tf_op jit(solution)/shard_map/ppermute | solution.py:289
  52.6 9.9 %collective-permute-start.18 = (bf16[128,512]{1,0:T(8,128)(2,1)S(1)}, bf16[128,512]{1,0:T(8,128)(2,1)S(1)}, u32[]{:S(2)}, u32[]{:S(2)}) collective-permute-start(bf16[128,512]{1,0:T(8,128)(2,1)S(1)} %get-tuple-element.54), channel_id=1, source_target_pairs={{8,0},{16,8},{24,16},{32,24},{40,32},{48,40},{56,48},{0,56},{9,1},... | collective-permute-start | bytes 393224 | tf_op jit(solution)/shard_map/ppermute | solution.py:290
  52.6 17.5 %collective-permute-start.21 = (bf16[128,512]{1,0:T(8,128)(2,1)S(1)}, bf16[128,512]{1,0:T(8,128)(2,1)S(1)}, u32[]{:S(2)}, u32[]{:S(2)}) collective-permute-start(bf16[128,512]{1,0:T(8,128)(2,1)S(1)} %get-tuple-element.55), channel_id=1, source_target_pairs={{32,0},{40,8},{48,16},{56,24},{0,32},{8,40},{16,48},{24,56},{33,1}... | collective-permute-start | bytes 393224 | tf_op jit(solution)/shard_map/ppermute | solution.py:292
  55.7 10.4 %collective-permute-start.16 = (bf16[128,512]{1,0:T(8,128)(2,1)S(1)}, bf16[128,512]{1,0:T(8,128)(2,1)S(1)}, u32[]{:S(2)}, u32[]{:S(2)}) collective-permute-start(bf16[128,512]{1,0:T(8,128)(2,1)S(1)} %add_convert_fusion.4), channel_id=1, source_target_pairs={{56,0},{0,8},{8,16},{16,24},{24,32},{32,40},{40,48},{48,56},{57,1}... | collective-permute-start | bytes 393224 | tf_op jit(solution)/shard_map/ppermute | solution.py:289
  62.6 6.6 %collective-permute-start.19 = (bf16[128,512]{1,0:T(8,128)(2,1)S(1)}, bf16[128,512]{1,0:T(8,128)(2,1)S(1)}, u32[]{:S(2)}, u32[]{:S(2)}) collective-permute-start(bf16[128,512]{1,0:T(8,128)(2,1)S(1)} %add_convert_fusion.2), channel_id=1, source_target_pairs={{8,0},{16,8},{24,16},{32,24},{40,32},{48,40},{56,48},{0,56},{9,1},... | collective-permute-start | bytes 393224 | tf_op jit(solution)/shard_map/ppermute | solution.py:290
  66.2 5.5 %collective-permute-start.17 = (bf16[128,512]{1,0:T(8,128)(2,1)S(1)}, bf16[128,512]{1,0:T(8,128)(2,1)S(1)}, u32[]{:S(2)}, u32[]{:S(2)}) collective-permute-start(bf16[128,512]{1,0:T(8,128)(2,1)S(1)} %add_convert_fusion.3), channel_id=1, source_target_pairs={{56,0},{0,8},{8,16},{16,24},{24,32},{32,40},{40,48},{48,56},{57,1}... | collective-permute-start | bytes 393224 | tf_op jit(solution)/shard_map/ppermute | solution.py:291
  69.2 6.3 %collective-permute-start.20 = (bf16[128,512]{1,0:T(8,128)(2,1)S(1)}, bf16[128,512]{1,0:T(8,128)(2,1)S(1)}, u32[]{:S(2)}, u32[]{:S(2)}) collective-permute-start(bf16[128,512]{1,0:T(8,128)(2,1)S(1)} %add_convert_fusion.1), channel_id=1, source_target_pairs={{8,0},{16,8},{24,16},{32,24},{40,32},{48,40},{56,48},{0,56},{9,1},... | collective-permute-start | bytes 393224 | tf_op jit(solution)/shard_map/ppermute | solution.py:291

commit v4 on v3

--- a/solution.py
+++ b/solution.py
@@ -280,7 +280,7 @@
     one, three = (lax.ppermute(new_weight, "x", ring(4, i)) for i in (1, 3))
     top = lax.ppermute(one[:HALF], "x", ring(4, 1))
     bottom = lax.ppermute(three[HALF:], "x", ring(4, 3))
-    near[1], top, bottom = lax.optimization_barrier((near[1], top, bottom))
+    near[2], top, bottom = lax.optimization_barrier((near[2], top, bottom))
     weights = [new_weight, one, top, bottom, three]
     far = [lax.ppermute(piece, "core", ring(2, 1)) for piece in near]
     parts = project_far(far[1:], *project_near(near, far[0], weights))

time: 76.3 us -> 74.5 us (0.976)
  starting transfers between devices: 48 us -> 43.2 us
  waiting for transfers between devices: 17.7 us -> 20.5 us
    ppermute x4, starting transfers between devices: 18.8 us -> 13.7 us  [body(): far = [lax.ppermute(piece, 'core', ring(2, 1)) for piece in near]]
    ppermute x3, waiting for transfers between devices: 1.24 us -> 5.15 us  [body(): near = [own] + [lax.ppermute(own, 'y', ring(4, j)) for j in (1, 2, 3)]]
    ppermute x3, starting transfers between devices: 3.33 us -> 5.16 us  [body(): near = [own] + [lax.ppermute(own, 'y', ring(4, j)) for j in (1, 2, 3)]]
    ppermute x1, starting transfers between devices: 3.77 us -> 2.33 us  [body(): top = lax.ppermute(one[:HALF], 'x', ring(4, 1))]
    ppermute x2, waiting for transfers between devices: 1.7 us -> 0.33 us  [body(): one, three = (lax.ppermute(new_weight, 'x', ring(4, i)) for i in (1, 3))]
    ppermute x2, starting transfers between devices: 9.05 us -> 7.92 us  [body(): up = add(near_up, lax.ppermute(up, 'z', ring(8, 7)))]
    ppermute x1, starting transfers between devices: 0.26 us -> 1.24 us  [body(): bottom = lax.ppermute(three[HALF:], 'x', ring(4, 3))]
where the time goes in v4:
time: 74.5 us; the launch traced here: 74.2 us
  starting transfers between devices  43.2 us (58%)
  waiting for transfers between devices  20.5 us (28%)
  Pallas kernels  6.85 us (9%)
  local copies, waits for them, and re-layouts  1.91 us (3%)
  other arithmetic  0.85 us (1%)
  between operations  0.78 us (1%)
    ppermute x4, starting transfers between devices, body(): far = [lax.ppermute(piece, 'core', ring(2, 1)) for piece in near]  13.7 us
    ppermute x2, starting transfers between devices, body(): up = add(near_up, lax.ppermute(up, 'z', ring(8, 7)))  7.92 us
    ppermute x3, starting transfers between devices, body(): near = [own] + [lax.ppermute(own, 'y', ring(4, j)) for j in (1, 2, 3)]  5.16 us
    ppermute x3, waiting for transfers between devices, body(): near = [own] + [lax.ppermute(own, 'y', ring(4, j)) for j in (1, 2, 3)]  5.15 us
    ppermute x2, starting transfers between devices, body(): one, three = (lax.ppermute(new_weight, 'x', ring(4, i)) for i in (1, 3))  4.78 us
    ppermute x2, waiting for transfers between devices, body(): up = add(near_up, lax.ppermute(up, 'z', ring(8, 7)))  4.32 us
    pallas_call x1, Pallas kernels, block_step(): pl.pallas_call(step_kernel, out_shape=(wide, wide, pltpu.VMEM((BLOCK, BLO...  4.11 us
    ppermute x1, waiting for transfers between devices, body(): lax.ppermute(down, 'z', ring(8, 1))  3.71 us
  transfers between devices with their start and end apart: 22, of which 10 were waited for; matrix products, arithmetic and copies ran while one was open for 1% of the time, Pallas kernels for 8%

profile of v4, /device:TPU:96, one launch (start us, length us, event | category | flops | bytes accessed | tf_op | source)
XLA Modules:
  0.0 74.2 jit_solution(2001189601249270867)
XLA Ops:
  0.6 1.0 %copy-done = bf16[128,2048]{1,0:T(8,128)(2,1)S(1)} copy-done((bf16[128,2048]{1,0:T(8,128)(2,1)S(1)}, bf16[128,2048]{1,0:T(8,128)(2,1)}, u32[]{:S(2)}) %copy-start) | copy-done | bytes 524312
  2.4 1.0 %collective-permute-start.1 = (bf16[128,512]{1,0:T(8,128)(2,1)S(1)}, bf16[128,512]{1,0:T(8,128)(2,1)S(1)}, u32[]{:S(2)}, u32[]{:S(2)}) collective-permute-start(bf16[128,512]{1,0:T(8,128)(2,1)S(1)} %get-tuple-element.34), channel_id=1, source_target_pairs={{0,8},{1,40},{8,16},{9,48},{16,24},{17,56},{24,0},{25,32},{32,9},{... | collective-permute-start | bytes 393224 | tf_op jit(solution)/shard_map/ppermute | solution.py:273
  4.5 4.1 %block_step.1 = (f32[512,512]{1,0:T(8,128)}, f32[512,512]{1,0:T(8,128)}, bf16[512,512]{1,0:T(8,128)(2,1)S(1)}, bf16[512,512]{1,0:T(8,128)(2,1)S(1)}) custom-call(s32[8,16]{1,0:T(8,128)} %bitcast.1, bf16[512,512]{1,0:T(8,128)(2,1)} %grad_hbm.1, bf16[512,512]{1,0:T(8,128)(2,1)} %weight_hbm.1, f32[512,512]{1,0:T(8,128)} %sl_hbm.1, f32[512,512]{1,0:T(8,128)} %sr_hbm.1, ...), custom_call_target="tpu_custom_call" | custom-call | flops 8053063680 | bytes 9437184 | tf_op jit(solution)/shard_map/block_step/pallas_call | solution.py:150
  8.6 1.6 %collective-permute-start.9 = (bf16[512,512]{1,0:T(8,128)(2,1)S(1)}, bf16[512,512]{1,0:T(8,128)(2,1)S(1)}, u32[]{:S(2)}, u32[]{:S(2)}) collective-permute-start(bf16[512,512]{1,0:T(8,128)(2,1)S(1)} %get-tuple-element.37.refs_5_), channel_id=1, source_target_pairs={{192,0},{0,64},{64,128},{128,192},{193,1},{1,65},{65,129},{129,193... | collective-permute-start | bytes 1572872 | tf_op jit(solution)/shard_map/ppermute | solution.py:280
  10.2 3.2 %collective-permute-start.7 = (bf16[512,512]{1,0:T(8,128)(2,1)S(1)}, bf16[512,512]{1,0:T(8,128)(2,1)S(1)}, u32[]{:S(2)}, u32[]{:S(2)}) collective-permute-start(bf16[512,512]{1,0:T(8,128)(2,1)S(1)} %get-tuple-element.37.refs_5_), channel_id=1, source_target_pairs={{64,0},{128,64},{192,128},{0,192},{65,1},{129,65},{193,129},{1,193... | collective-permute-start | bytes 1572872 | tf_op jit(solution)/shard_map/ppermute | solution.py:280
  13.4 1.5 %collective-permute-done.2 = bf16[128,512]{1,0:T(8,128)(2,1)S(1)} collective-permute-done((bf16[128,512]{1,0:T(8,128)(2,1)S(1)}, bf16[128,512]{1,0:T(8,128)(2,1)S(1)}, u32[]{:S(2)}, u32[]{:S(2)}) %collective-permute-start.2) | collective-permute-done | bytes 131104 | tf_op jit(solution)/shard_map/ppermute | solution.py:273
  15.0 1.9 %collective-permute-start.6 = (bf16[512,512]{1,0:T(8,128)(2,1)S(1)}, bf16[512,512]{1,0:T(8,128)(2,1)S(1)}, u32[]{:S(2)}, u32[]{:S(2)}) collective-permute-start(bf16[512,512]{1,0:T(8,128)(2,1)S(1)} %constant_dynamic-update-slice_fusion.refs_0_), channel_id=1, source_target_pairs={{4,0},{6,2},{0,4},{2,6},{5,1},{7,3},{1,5},{3,7},{12,8},{14,10},{8,... | collective-permute-start | bytes 1572872 | tf_op jit(solution)/shard_map/ppermute | solution.py:279
  17.8 2.3 %collective-permute-start.4 = (bf16[512,512]{1,0:T(8,128)(2,1)S(1)}, bf16[512,512]{1,0:T(8,128)(2,1)S(1)}, u32[]{:S(2)}, u32[]{:S(2)}) collective-permute-start(bf16[512,512]{1,0:T(8,128)(2,1)S(1)} %constant_dynamic-update-slice_fusion.refs_0_), channel_id=1, source_target_pairs={{2,0},{4,2},{6,4},{0,6},{3,1},{5,3},{7,5},{1,7},{10,8},{12,10},{14... | collective-permute-start | bytes 1572872 | tf_op jit(solution)/shard_map/ppermute | solution.py:279
  20.5 1.2 %collective-permute-start.10 = (bf16[256,512]{1,0:T(8,128)(2,1)S(1)}, bf16[256,512]{1,0:T(8,128)(2,1)S(1)}, u32[]{:S(2)}, u32[]{:S(2)}) collective-permute-start(bf16[256,512]{1,0:T(8,128)(2,1)S(1)} %slice.9), channel_id=1, source_target_pairs={{192,0},{0,64},{64,128},{128,192},{193,1},{1,65},{65,129},{129,193... | collective-permute-start | bytes 786440 | tf_op jit(solution)/shard_map/ppermute | solution.py:282
  21.7 2.3 %collective-permute-start.8 = (bf16[256,512]{1,0:T(8,128)(2,1)S(1)}, bf16[256,512]{1,0:T(8,128)(2,1)S(1)}, u32[]{:S(2)}, u32[]{:S(2)}) collective-permute-start(bf16[256,512]{1,0:T(8,128)(2,1)S(1)} %slice.8), channel_id=1, source_target_pairs={{64,0},{128,64},{192,128},{0,192},{65,1},{129,65},{193,129},{1,193... | collective-permute-start | bytes 786440 | tf_op jit(solution)/shard_map/ppermute | solution.py:281
  24.1 1.8 %collective-permute-done.6.refs_2_ = bf16[512,512]{1,0:T(8,128)(2,1)S(1)} collective-permute-done((bf16[512,512]{1,0:T(8,128)(2,1)S(1)}, bf16[512,512]{1,0:T(8,128)(2,1)S(1)}, u32[]{:S(2)}, u32[]{:S(2)}) %collective-permute-start.6) | collective-permute-done | bytes 524320 | tf_op jit(solution)/shard_map/ppermute | solution.py:279
  25.8 11.1 %collective-permute-start.14 = (bf16[512,512]{1,0:T(8,128)(2,1)S(1)}, bf16[512,512]{1,0:T(8,128)(2,1)S(1)}, u32[]{:S(2)}, u32[]{:S(2)}) collective-permute-start(bf16[512,512]{1,0:T(8,128)(2,1)S(1)} %constant_dynamic-update-slice_fusion.refs_0_), channel_id=1, source_target_pairs={{1,0},{0,1},{3,2},{2,3},{5,4},{4,5},{7,6},{6,7},{9,8},{8,9},{11,10... | collective-permute-start | bytes 1572872 | tf_op jit(solution)/shard_map/ppermute | solution.py:285
  36.9 3.4 %collective-permute-done.12.refs_3_ = bf16[512,512]{1,0:T(8,128)(2,1)S(1)} collective-permute-done((bf16[512,512]{1,0:T(8,128)(2,1)S(1)}, bf16[512,512]{1,0:T(8,128)(2,1)S(1)}, u32[]{:S(2)}, u32[]{:S(2)}) %collective-permute-start.12) | collective-permute-done | bytes 524320 | tf_op jit(solution)/shard_map/ppermute | solution.py:279
  40.3 2.1 %collective-permute-start.13 = (bf16[512,512]{1,0:T(8,128)(2,1)S(1)}, bf16[512,512]{1,0:T(8,128)(2,1)S(1)}, u32[]{:S(2)}, u32[]{:S(2)}) collective-permute-start(bf16[512,512]{1,0:T(8,128)(2,1)S(1)} %collective-permute-done.12.refs_3_), channel_id=1, source_target_pairs={{1,0},{0,1},{3,2},{2,3},{5,4},{4,5},{7,6},{6,7},{9,8},{8,9},{11,10... | collective-permute-start | bytes 1572872 | tf_op jit(solution)/shard_map/ppermute | solution.py:285
  42.9 1.7 %project_near.1 = (f32[512,512]{1,0:T(8,128)S(1)}, f32[512,512]{1,0:T(8,128)S(1)}, bf16[4,512,512]{2,1,0:T(8,128)(2,1)S(1)}) custom-call(bf16[512,512]{1,0:T(8,128)(2,1)S(1)} %constant_dynamic-update-slice_fusion.refs_0_, bf16[512,512]{1,0:T(8,128)(2,1)S(1)} %collective-permute-done.4.refs_1_, bf16[512,512]{1,0:T(8,128)(2,1)S(1)} %collective-permute-done.6.refs_2_, ...), custom_call_target="tpu_custom_call" | custom-call | flops 1073741824 | bytes 7340032 | tf_op jit(solution)/shard_map/project_near/pallas_call | solution.py:217
  45.4 1.0 %project_far.1 = (f32[128,512]{1,0:T(8,128)S(1)}, bf16[128,512]{1,0:T(8,128)(2,1)S(1)}, bf16[128,512]{1,0:T(8,128)(2,1)S(1)}, bf16[128,512]{1,0:T(8,128)(2,1)S(1...) custom-call(bf16[512,512]{1,0:T(8,128)(2,1)S(1)} %collective-permute, ...), custom_call_target="tpu_custom_call" | custom-call | flops 1073741824 | bytes 7340032 | tf_op jit(solution)/shard_map/project_far/pallas_call | solution.py:244
  46.4 4.1 %collective-permute-start.15 = (bf16[128,512]{1,0:T(8,128)(2,1)S(1)}, bf16[128,512]{1,0:T(8,128)(2,1)S(1)}, u32[]{:S(2)}, u32[]{:S(2)}) collective-permute-start(bf16[128,512]{1,0:T(8,128)(2,1)S(1)} %get-tuple-element.51), channel_id=1, source_target_pairs={{56,0},{0,8},{8,16},{16,24},{24,32},{32,40},{40,48},{48,56},{57,1}... | collective-permute-start | bytes 393224 | tf_op jit(solution)/shard_map/ppermute | solution.py:289
  50.6 2.2 %collective-permute-start.21 = (bf16[128,512]{1,0:T(8,128)(2,1)S(1)}, bf16[128,512]{1,0:T(8,128)(2,1)S(1)}, u32[]{:S(2)}, u32[]{:S(2)}) collective-permute-start(bf16[128,512]{1,0:T(8,128)(2,1)S(1)} %get-tuple-element.55), channel_id=1, source_target_pairs={{32,0},{40,8},{48,16},{56,24},{0,32},{8,40},{16,48},{24,56},{33,1}... | collective-permute-start | bytes 393224 | tf_op jit(solution)/shard_map/ppermute | solution.py:292
  53.7 3.8 %collective-permute-start.16 = (bf16[128,512]{1,0:T(8,128)(2,1)S(1)}, bf16[128,512]{1,0:T(8,128)(2,1)S(1)}, u32[]{:S(2)}, u32[]{:S(2)}) collective-permute-start(bf16[128,512]{1,0:T(8,128)(2,1)S(1)} %add_convert_fusion.4), channel_id=1, source_target_pairs={{56,0},{0,8},{8,16},{16,24},{24,32},{32,40},{40,48},{48,56},{57,1}... | collective-permute-start | bytes 393224 | tf_op jit(solution)/shard_map/ppermute | solution.py:289
  57.5 3.1 %collective-permute-done.18 = bf16[128,512]{1,0:T(8,128)(2,1)S(1)} collective-permute-done((bf16[128,512]{1,0:T(8,128)(2,1)S(1)}, bf16[128,512]{1,0:T(8,128)(2,1)S(1)}, u32[]{:S(2)}, u32[]{:S(2)}) %collective-permute-start.18) | collective-permute-done | bytes 131104 | tf_op jit(solution)/shard_map/ppermute | solution.py:290
  60.7 3.5 %collective-permute-done.16 = bf16[128,512]{1,0:T(8,128)(2,1)S(1)} collective-permute-done((bf16[128,512]{1,0:T(8,128)(2,1)S(1)}, bf16[128,512]{1,0:T(8,128)(2,1)S(1)}, u32[]{:S(2)}, u32[]{:S(2)}) %collective-permute-start.16) | collective-permute-done | bytes 131104 | tf_op jit(solution)/shard_map/ppermute | solution.py:289
  64.2 3.0 %collective-permute-start.17 = (bf16[128,512]{1,0:T(8,128)(2,1)S(1)}, bf16[128,512]{1,0:T(8,128)(2,1)S(1)}, u32[]{:S(2)}, u32[]{:S(2)}) collective-permute-start(bf16[128,512]{1,0:T(8,128)(2,1)S(1)} %add_convert_fusion.3), channel_id=1, source_target_pairs={{56,0},{0,8},{8,16},{16,24},{24,32},{32,40},{40,48},{48,56},{57,1}... | collective-permute-start | bytes 393224 | tf_op jit(solution)/shard_map/ppermute | solution.py:291
  68.1 1.7 %collective-permute-done.17 = bf16[128,512]{1,0:T(8,128)(2,1)S(1)} collective-permute-done((bf16[128,512]{1,0:T(8,128)(2,1)S(1)}, bf16[128,512]{1,0:T(8,128)(2,1)S(1)}, u32[]{:S(2)}, u32[]{:S(2)}) %collective-permute-start.17) | collective-permute-done | bytes 131104 | tf_op jit(solution)/shard_map/ppermute | solution.py:291
  69.7 3.7 %collective-permute-done.20 = bf16[128,512]{1,0:T(8,128)(2,1)S(1)} collective-permute-done((bf16[128,512]{1,0:T(8,128)(2,1)S(1)}, bf16[128,512]{1,0:T(8,128)(2,1)S(1)}, u32[]{:S(2)}, u32[]{:S(2)}) %collective-permute-start.20) | collective-permute-done | bytes 131104 | tf_op jit(solution)/shard_map/ppermute | solution.py:291
  (38 shorter events, 7.1 us)
Async XLA Ops:
  0.6 1.0 %copy-start = (bf16[128,2048]{1,0:T(8,128)(2,1)S(1)}, bf16[128,2048]{1,0:T(8,128)(2,1)}, u32[]{:S(2)}) copy-start(bf16[128,2048]{1,0:T(8,128)(2,1)} %hidden.1) | copy-start | bytes 1572868
  1.7 8.5 %collective-permute-start = (bf16[128,512]{1,0:T(8,128)(2,1)S(1)}, bf16[128,512]{1,0:T(8,128)(2,1)S(1)}, u32[]{:S(2)}, u32[]{:S(2)}) collective-permute-start(bf16[128,512]{1,0:T(8,128)(2,1)S(1)} %get-tuple-element.33), channel_id=1, source_target_pairs={{0,0},{1,32},{8,8},{9,40},{16,16},{17,48},{24,24},{25,56},{32,1},{... | collective-permute-start | bytes 393224 | tf_op jit(solution)/shard_map/ppermute | solution.py:273
  2.4 11.0 %collective-permute-start.1 = (bf16[128,512]{1,0:T(8,128)(2,1)S(1)}, bf16[128,512]{1,0:T(8,128)(2,1)S(1)}, u32[]{:S(2)}, u32[]{:S(2)}) collective-permute-start(bf16[128,512]{1,0:T(8,128)(2,1)S(1)} %get-tuple-element.34), channel_id=1, source_target_pairs={{0,8},{1,40},{8,16},{9,48},{16,24},{17,56},{24,0},{25,32},{32,9},{... | collective-permute-start | bytes 393224 | tf_op jit(solution)/shard_map/ppermute | solution.py:273
  3.4 11.5 %collective-permute-start.2 = (bf16[128,512]{1,0:T(8,128)(2,1)S(1)}, bf16[128,512]{1,0:T(8,128)(2,1)S(1)}, u32[]{:S(2)}, u32[]{:S(2)}) collective-permute-start(bf16[128,512]{1,0:T(8,128)(2,1)S(1)} %get-tuple-element.35), channel_id=1, source_target_pairs={{0,16},{1,48},{8,24},{9,56},{16,0},{17,32},{24,8},{25,40},{32,17},... | collective-permute-start | bytes 393224 | tf_op jit(solution)/shard_map/ppermute | solution.py:273
  4.0 10.9 %collective-permute-start.3 = (bf16[128,512]{1,0:T(8,128)(2,1)S(1)}, bf16[128,512]{1,0:T(8,128)(2,1)S(1)}, u32[]{:S(2)}, u32[]{:S(2)}) collective-permute-start(bf16[128,512]{1,0:T(8,128)(2,1)S(1)} %get-tuple-element.36), channel_id=1, source_target_pairs={{0,24},{1,56},{8,0},{9,32},{16,8},{17,40},{24,16},{25,48},{32,25},... | collective-permute-start | bytes 393224 | tf_op jit(solution)/shard_map/ppermute | solution.py:273
  8.6 11.8 %collective-permute-start.9 = (bf16[512,512]{1,0:T(8,128)(2,1)S(1)}, bf16[512,512]{1,0:T(8,128)(2,1)S(1)}, u32[]{:S(2)}, u32[]{:S(2)}) collective-permute-start(bf16[512,512]{1,0:T(8,128)(2,1)S(1)} %get-tuple-element.37.refs_5_), channel_id=1, source_target_pairs={{192,0},{0,64},{64,128},{128,192},{193,1},{1,65},{65,129},{129,193... | collective-permute-start | bytes 1572872 | tf_op jit(solution)/shard_map/ppermute | solution.py:280
  10.2 11.5 %collective-permute-start.7 = (bf16[512,512]{1,0:T(8,128)(2,1)S(1)}, bf16[512,512]{1,0:T(8,128)(2,1)S(1)}, u32[]{:S(2)}, u32[]{:S(2)}) collective-permute-start(bf16[512,512]{1,0:T(8,128)(2,1)S(1)} %get-tuple-element.37.refs_5_), channel_id=1, source_target_pairs={{64,0},{128,64},{192,128},{0,192},{65,1},{129,65},{193,129},{1,193... | collective-permute-start | bytes 1572872 | tf_op jit(solution)/shard_map/ppermute | solution.py:280
  15.0 10.9 %collective-permute-start.6 = (bf16[512,512]{1,0:T(8,128)(2,1)S(1)}, bf16[512,512]{1,0:T(8,128)(2,1)S(1)}, u32[]{:S(2)}, u32[]{:S(2)}) collective-permute-start(bf16[512,512]{1,0:T(8,128)(2,1)S(1)} %constant_dynamic-update-slice_fusion.refs_0_), channel_id=1, source_target_pairs={{4,0},{6,2},{0,4},{2,6},{5,1},{7,3},{1,5},{3,7},{12,8},{14,10},{8,... | collective-permute-start | bytes 1572872 | tf_op jit(solution)/shard_map/ppermute | solution.py:279
  16.9 23.4 %collective-permute-start.12 = (bf16[512,512]{1,0:T(8,128)(2,1)S(1)}, bf16[512,512]{1,0:T(8,128)(2,1)S(1)}, u32[]{:S(2)}, u32[]{:S(2)}) collective-permute-start(bf16[512,512]{1,0:T(8,128)(2,1)S(1)} %constant_dynamic-update-slice_fusion.refs_0_), channel_id=1, source_target_pairs={{6,0},{0,2},{2,4},{4,6},{7,1},{1,3},{3,5},{5,7},{14,8},{8,10},{10,... | collective-permute-start | bytes 1572872 | tf_op jit(solution)/shard_map/ppermute | solution.py:279
  17.8 24.6 %collective-permute-start.4 = (bf16[512,512]{1,0:T(8,128)(2,1)S(1)}, bf16[512,512]{1,0:T(8,128)(2,1)S(1)}, u32[]{:S(2)}, u32[]{:S(2)}) collective-permute-start(bf16[512,512]{1,0:T(8,128)(2,1)S(1)} %constant_dynamic-update-slice_fusion.refs_0_), channel_id=1, source_target_pairs={{2,0},{4,2},{6,4},{0,6},{3,1},{5,3},{7,5},{1,7},{10,8},{12,10},{14... | collective-permute-start | bytes 1572872 | tf_op jit(solution)/shard_map/ppermute | solution.py:279
  20.5 21.9 %collective-permute-start.10 = (bf16[256,512]{1,0:T(8,128)(2,1)S(1)}, bf16[256,512]{1,0:T(8,128)(2,1)S(1)}, u32[]{:S(2)}, u32[]{:S(2)}) collective-permute-start(bf16[256,512]{1,0:T(8,128)(2,1)S(1)} %slice.9), channel_id=1, source_target_pairs={{192,0},{0,64},{64,128},{128,192},{193,1},{1,65},{65,129},{129,193... | collective-permute-start | bytes 786440 | tf_op jit(solution)/shard_map/ppermute | solution.py:282
  21.7 20.7 %collective-permute-start.8 = (bf16[256,512]{1,0:T(8,128)(2,1)S(1)}, bf16[256,512]{1,0:T(8,128)(2,1)S(1)}, u32[]{:S(2)}, u32[]{:S(2)}) collective-permute-start(bf16[256,512]{1,0:T(8,128)(2,1)S(1)} %slice.8), channel_id=1, source_target_pairs={{64,0},{128,64},{192,128},{0,192},{65,1},{129,65},{193,129},{1,193... | collective-permute-start | bytes 786440 | tf_op jit(solution)/shard_map/ppermute | solution.py:281
  25.8 17.1 %collective-permute-start.14 = (bf16[512,512]{1,0:T(8,128)(2,1)S(1)}, bf16[512,512]{1,0:T(8,128)(2,1)S(1)}, u32[]{:S(2)}, u32[]{:S(2)}) collective-permute-start(bf16[512,512]{1,0:T(8,128)(2,1)S(1)} %constant_dynamic-update-slice_fusion.refs_0_), channel_id=1, source_target_pairs={{1,0},{0,1},{3,2},{2,3},{5,4},{4,5},{7,6},{6,7},{9,8},{8,9},{11,10... | collective-permute-start | bytes 1572872 | tf_op jit(solution)/shard_map/ppermute | solution.py:285
  40.3 4.4 %collective-permute-start.13 = (bf16[512,512]{1,0:T(8,128)(2,1)S(1)}, bf16[512,512]{1,0:T(8,128)(2,1)S(1)}, u32[]{:S(2)}, u32[]{:S(2)}) collective-permute-start(bf16[512,512]{1,0:T(8,128)(2,1)S(1)} %collective-permute-done.12.refs_3_), channel_id=1, source_target_pairs={{1,0},{0,1},{3,2},{2,3},{5,4},{4,5},{7,6},{6,7},{9,8},{8,9},{11,10... | collective-permute-start | bytes 1572872 | tf_op jit(solution)/shard_map/ppermute | solution.py:285
  42.4 2.3 %collective-permute-start.5 = (bf16[512,512]{1,0:T(8,128)(2,1)S(1)}, bf16[512,512]{1,0:T(8,128)(2,1)S(1)}, u32[]{:S(2)}, u32[]{:S(2)}) collective-permute-start(bf16[512,512]{1,0:T(8,128)(2,1)S(1)} %collective-permute-done.4.refs_1_), channel_id=1, source_target_pairs={{1,0},{0,1},{3,2},{2,3},{5,4},{4,5},{7,6},{6,7},{9,8},{8,9},{11,10... | collective-permute-start | bytes 1572872 | tf_op jit(solution)/shard_map/ppermute | solution.py:285
  42.4 3.0 %collective-permute-start.11 = (bf16[512,512]{1,0:T(8,128)(2,1)S(1)}, bf16[512,512]{1,0:T(8,128)(2,1)S(1)}, u32[]{:S(2)}, u32[]{:S(2)}) collective-permute-start(bf16[512,512]{1,0:T(8,128)(2,1)S(1)} %collective-permute-done.6.refs_2_), channel_id=1, source_target_pairs={{1,0},{0,1},{3,2},{2,3},{5,4},{4,5},{7,6},{6,7},{9,8},{8,9},{11,10... | collective-permute-start | bytes 1572872 | tf_op jit(solution)/shard_map/ppermute | solution.py:285
  46.4 7.2 %collective-permute-start.15 = (bf16[128,512]{1,0:T(8,128)(2,1)S(1)}, bf16[128,512]{1,0:T(8,128)(2,1)S(1)}, u32[]{:S(2)}, u32[]{:S(2)}) collective-permute-start(bf16[128,512]{1,0:T(8,128)(2,1)S(1)} %get-tuple-element.51), channel_id=1, source_target_pairs={{56,0},{0,8},{8,16},{16,24},{24,32},{32,40},{40,48},{48,56},{57,1}... | collective-permute-start | bytes 393224 | tf_op jit(solution)/shard_map/ppermute | solution.py:289
  50.6 9.9 %collective-permute-start.18 = (bf16[128,512]{1,0:T(8,128)(2,1)S(1)}, bf16[128,512]{1,0:T(8,128)(2,1)S(1)}, u32[]{:S(2)}, u32[]{:S(2)}) collective-permute-start(bf16[128,512]{1,0:T(8,128)(2,1)S(1)} %get-tuple-element.54), channel_id=1, source_target_pairs={{8,0},{16,8},{24,16},{32,24},{40,32},{48,40},{56,48},{0,56},{9,1},... | collective-permute-start | bytes 393224 | tf_op jit(solution)/shard_map/ppermute | solution.py:290
  50.6 17.5 %collective-permute-start.21 = (bf16[128,512]{1,0:T(8,128)(2,1)S(1)}, bf16[128,512]{1,0:T(8,128)(2,1)S(1)}, u32[]{:S(2)}, u32[]{:S(2)}) collective-permute-start(bf16[128,512]{1,0:T(8,128)(2,1)S(1)} %get-tuple-element.55), channel_id=1, source_target_pairs={{32,0},{40,8},{48,16},{56,24},{0,32},{8,40},{16,48},{24,56},{33,1}... | collective-permute-start | bytes 393224 | tf_op jit(solution)/shard_map/ppermute | solution.py:292
  53.7 10.4 %collective-permute-start.16 = (bf16[128,512]{1,0:T(8,128)(2,1)S(1)}, bf16[128,512]{1,0:T(8,128)(2,1)S(1)}, u32[]{:S(2)}, u32[]{:S(2)}) collective-permute-start(bf16[128,512]{1,0:T(8,128)(2,1)S(1)} %add_convert_fusion.4), channel_id=1, source_target_pairs={{56,0},{0,8},{8,16},{16,24},{24,32},{32,40},{40,48},{48,56},{57,1}... | collective-permute-start | bytes 393224 | tf_op jit(solution)/shard_map/ppermute | solution.py:289
  60.6 6.6 %collective-permute-start.19 = (bf16[128,512]{1,0:T(8,128)(2,1)S(1)}, bf16[128,512]{1,0:T(8,128)(2,1)S(1)}, u32[]{:S(2)}, u32[]{:S(2)}) collective-permute-start(bf16[128,512]{1,0:T(8,128)(2,1)S(1)} %add_convert_fusion.2), channel_id=1, source_target_pairs={{8,0},{16,8},{24,16},{32,24},{40,32},{48,40},{56,48},{0,56},{9,1},... | collective-permute-start | bytes 393224 | tf_op jit(solution)/shard_map/ppermute | solution.py:290
  64.2 5.6 %collective-permute-start.17 = (bf16[128,512]{1,0:T(8,128)(2,1)S(1)}, bf16[128,512]{1,0:T(8,128)(2,1)S(1)}, u32[]{:S(2)}, u32[]{:S(2)}) collective-permute-start(bf16[128,512]{1,0:T(8,128)(2,1)S(1)} %add_convert_fusion.3), channel_id=1, source_target_pairs={{56,0},{0,8},{8,16},{16,24},{24,32},{32,40},{40,48},{48,56},{57,1}... | collective-permute-start | bytes 393224 | tf_op jit(solution)/shard_map/ppermute | solution.py:291
  67.2 6.3 %collective-permute-start.20 = (bf16[128,512]{1,0:T(8,128)(2,1)S(1)}, bf16[128,512]{1,0:T(8,128)(2,1)S(1)}, u32[]{:S(2)}, u32[]{:S(2)}) collective-permute-start(bf16[128,512]{1,0:T(8,128)(2,1)S(1)} %add_convert_fusion.1), channel_id=1, source_target_pairs={{8,0},{16,8},{24,16},{32,24},{40,32},{48,40},{56,48},{0,56},{9,1},... | collective-permute-start | bytes 393224 | tf_op jit(solution)/shard_map/ppermute | solution.py:291

commit v5 on v4

--- a/solution.py
+++ b/solution.py
@@ -1,3 +1,5 @@
+import functools
+
 import jax
 import jax.numpy as jnp
 from jax import lax
@@ -12,6 +14,7 @@
 KEEP = 0.75
 STEP = 0.003
 FLOOR = 1e-06
+SENDS = {(1, 3): (3, 7, 1, 5), (0, 2): (0, 4, 2, 6)}
 F32 = jnp.float32
 BF16 = jnp.bfloat16
 HBM = pl.BlockSpec(memory_space=pltpu.HBM)
@@ -228,30 +231,34 @@
     )(*[vmem(one) for one in (*near, far, *weights)])
 
 
-def far_kernel(*refs):
-    far, near_sum, far_part, placed, outs = refs[0:3], refs[3], refs[4], refs[5], refs[6:14]
-    z, core = lax.axis_index("z"), lax.axis_index("core")
-    far_sum = multiply(far_part[...], far, placed)
-    for s in range(8):
-        piece = -s % 4
-        rows = slice(piece * ROWS, (piece + 1) * ROWS)
+def far_kernel(pieces, *refs):
+    far, near_sum, far_part, placed, outs = refs[0:3], refs[3], refs[4], refs[5], refs[6:10]
+    z, y, core = lax.axis_index("z"), lax.axis_index("y"), lax.axis_index("core")
+    rows = [slice(piece * ROWS, (piece + 1) * ROWS) for piece in pieces]
+    acc = jnp.concatenate([far_part[one] for one in rows], axis=0)
+    for j in range(1, 4):
+        acc += mm(jnp.concatenate([far[j - 1][one] for one in rows], axis=0), placed[(y + j) % 4])
+    for k, s in enumerate(SENDS[pieces]):
+        i = pieces.index(-s % 4)
         is_near = ((z + s) % 8) // 4 == core
-        outs[s][...] = jnp.where(is_near, near_sum[rows], far_sum[rows]).astype(outs[s].dtype)
-
-
-def project_far(far, near_sum, far_part, placed):
-    part = pltpu.VMEM((ROWS, BLOCK), BF16)
-    return pl.pallas_call(
-        far_kernel,
-        out_shape=(pltpu.VMEM((ROWS, BLOCK), F32),) + (part,) * 7,
+        part = jnp.where(is_near, near_sum[rows[i]], acc[i * ROWS : (i + 1) * ROWS])
+        outs[k][...] = part.astype(outs[k].dtype)
+
+
+def project_far(pieces, far, near_sum, far_part, placed):
+    kinds = [F32 if s == 0 else BF16 for s in SENDS[pieces]]
+    parts = pl.pallas_call(
+        functools.partial(far_kernel, pieces),
+        out_shape=tuple(pltpu.VMEM((ROWS, BLOCK), kind) for kind in kinds),
         in_specs=[VMEM] * 6,
-        out_specs=(VMEM,) * 8,
+        out_specs=(VMEM,) * 4,
         compiler_params=pltpu.CompilerParams(vmem_limit_bytes=16 * 1024 * 1024),
         cost_estimate=pl.CostEstimate(
-            flops=2 * 512 * 2048 * BLOCK, bytes_accessed=7 * 1024 * 1024, transcendentals=0
+            flops=2 * 256 * 1536 * BLOCK, bytes_accessed=4 * 1024 * 1024, transcendentals=0
         ),
         name="project_far",
     )(*[vmem(one) for one in (*far, near_sum, far_part, placed)])
+    return dict(zip(SENDS[pieces], parts))
 
 
 def ring(size, shift):
@@ -283,7 +290,8 @@
     near[2], top, bottom = lax.optimization_barrier((near[2], top, bottom))
     weights = [new_weight, one, top, bottom, three]
     far = [lax.ppermute(piece, "core", ring(2, 1)) for piece in near]
-    parts = project_far(far[1:], *project_near(near, far[0], weights))
+    sums = project_near(near, far[0], weights)
+    parts = project_far((1, 3), far[1:], *sums) | project_far((0, 2), far[1:], *sums)
     up, down = parts[3], parts[5]
     for near_up, near_down in ((parts[2], parts[6]), (parts[1], parts[7])):
         up = add(near_up, lax.ppermute(up, "z", ring(8, 7)))

time: 74.5 us -> 74.6 us (level)
    ppermute x2, waiting for transfers between devices: 4.32 us -> 7.39 us  [body(): up = add(near_up, lax.ppermute(up, 'z', ring(8, 7)))]
    ppermute x2, waiting for transfers between devices: 3.08 us -> 0.01 us  [body(): down = add(near_down, lax.ppermute(down, 'z', ring(8, 1)))]
  transfers between devices with their start and end apart: 22 -> 22, of which waited for: 10 -> 9; matrix products, arithmetic and copies ran while one was open for 1% -> 1% of each run, Pallas kernels for 8% -> 9%
where the time goes in v5:
time: 74.6 us; the launch traced here: 74.2 us
  starting transfers between devices  43.1 us (58%)
  waiting for transfers between devices  20.5 us (27%)
  Pallas kernels  7.02 us (9%)
  local copies, waits for them, and re-layouts  1.91 us (3%)
  other arithmetic  0.85 us (1%)
  between operations  0.79 us (1%)
    ppermute x4, starting transfers between devices, body(): far = [lax.ppermute(piece, 'core', ring(2, 1)) for piece in near]  13.7 us
    ppermute x2, starting transfers between devices, body(): up = add(near_up, lax.ppermute(up, 'z', ring(8, 7)))  7.92 us
    ppermute x2, waiting for transfers between devices, body(): up = add(near_up, lax.ppermute(up, 'z', ring(8, 7)))  7.39 us
    ppermute x3, starting transfers between devices, body(): near = [own] + [lax.ppermute(own, 'y', ring(4, j)) for j in (1, 2, 3)]  5.16 us
    ppermute x3, waiting for transfers between devices, body(): near = [own] + [lax.ppermute(own, 'y', ring(4, j)) for j in (1, 2, 3)]  5.15 us
    ppermute x2, starting transfers between devices, body(): one, three = (lax.ppermute(new_weight, 'x', ring(4, i)) for i in (1, 3))  4.78 us
    pallas_call x1, Pallas kernels, block_step(): pl.pallas_call(step_kernel, out_shape=(wide, wide, pltpu.VMEM((BLOCK, BLO...  4.11 us
    ppermute x1, waiting for transfers between devices, body(): lax.ppermute(down, 'z', ring(8, 1))  3.48 us
  transfers between devices with their start and end apart: 22, of which 9 were waited for; matrix products, arithmetic and copies ran while one was open for 1% of the time, Pallas kernels for 9%

profile of v5, /device:TPU:96, one launch (start us, length us, event | category | flops | bytes accessed | tf_op | source)
XLA Modules:
  0.0 74.2 jit_solution(2993648090833111523)
XLA Ops:
  0.6 1.0 %copy-done = bf16[128,2048]{1,0:T(8,128)(2,1)S(1)} copy-done((bf16[128,2048]{1,0:T(8,128)(2,1)S(1)}, bf16[128,2048]{1,0:T(8,128)(2,1)}, u32[]{:S(2)}) %copy-start) | copy-done | bytes 524312
  2.4 1.0 %collective-permute-start.1 = (bf16[128,512]{1,0:T(8,128)(2,1)S(1)}, bf16[128,512]{1,0:T(8,128)(2,1)S(1)}, u32[]{:S(2)}, u32[]{:S(2)}) collective-permute-start(bf16[128,512]{1,0:T(8,128)(2,1)S(1)} %get-tuple-element.34), channel_id=1, source_target_pairs={{0,8},{1,40},{8,16},{9,48},{16,24},{17,56},{24,0},{25,32},{32,9},{... | collective-permute-start | bytes 393224 | tf_op jit(solution)/shard_map/ppermute | solution.py:280
  4.5 4.1 %block_step.1 = (f32[512,512]{1,0:T(8,128)}, f32[512,512]{1,0:T(8,128)}, bf16[512,512]{1,0:T(8,128)(2,1)S(1)}, bf16[512,512]{1,0:T(8,128)(2,1)S(1)}) custom-call(s32[8,16]{1,0:T(8,128)} %bitcast.1, bf16[512,512]{1,0:T(8,128)(2,1)} %grad_hbm.1, bf16[512,512]{1,0:T(8,128)(2,1)} %weight_hbm.1, f32[512,512]{1,0:T(8,128)} %sl_hbm.1, f32[512,512]{1,0:T(8,128)} %sr_hbm.1, ...), custom_call_target="tpu_custom_call" | custom-call | flops 8053063680 | bytes 9437184 | tf_op jit(solution)/shard_map/block_step/pallas_call | solution.py:153
  8.6 1.6 %collective-permute-start.9 = (bf16[512,512]{1,0:T(8,128)(2,1)S(1)}, bf16[512,512]{1,0:T(8,128)(2,1)S(1)}, u32[]{:S(2)}, u32[]{:S(2)}) collective-permute-start(bf16[512,512]{1,0:T(8,128)(2,1)S(1)} %get-tuple-element.37.refs_5_), channel_id=1, source_target_pairs={{192,0},{0,64},{64,128},{128,192},{193,1},{1,65},{65,129},{129,193... | collective-permute-start | bytes 1572872 | tf_op jit(solution)/shard_map/ppermute | solution.py:287
  10.2 3.2 %collective-permute-start.7 = (bf16[512,512]{1,0:T(8,128)(2,1)S(1)}, bf16[512,512]{1,0:T(8,128)(2,1)S(1)}, u32[]{:S(2)}, u32[]{:S(2)}) collective-permute-start(bf16[512,512]{1,0:T(8,128)(2,1)S(1)} %get-tuple-element.37.refs_5_), channel_id=1, source_target_pairs={{64,0},{128,64},{192,128},{0,192},{65,1},{129,65},{193,129},{1,193... | collective-permute-start | bytes 1572872 | tf_op jit(solution)/shard_map/ppermute | solution.py:287
  13.4 1.5 %collective-permute-done.2 = bf16[128,512]{1,0:T(8,128)(2,1)S(1)} collective-permute-done((bf16[128,512]{1,0:T(8,128)(2,1)S(1)}, bf16[128,512]{1,0:T(8,128)(2,1)S(1)}, u32[]{:S(2)}, u32[]{:S(2)}) %collective-permute-start.2) | collective-permute-done | bytes 131104 | tf_op jit(solution)/shard_map/ppermute | solution.py:280
  15.0 1.9 %collective-permute-start.6 = (bf16[512,512]{1,0:T(8,128)(2,1)S(1)}, bf16[512,512]{1,0:T(8,128)(2,1)S(1)}, u32[]{:S(2)}, u32[]{:S(2)}) collective-permute-start(bf16[512,512]{1,0:T(8,128)(2,1)S(1)} %constant_dynamic-update-slice_fusion.refs_0_), channel_id=1, source_target_pairs={{4,0},{6,2},{0,4},{2,6},{5,1},{7,3},{1,5},{3,7},{12,8},{14,10},{8,... | collective-permute-start | bytes 1572872 | tf_op jit(solution)/shard_map/ppermute | solution.py:286
  17.6 2.6 %collective-permute-start.4 = (bf16[512,512]{1,0:T(8,128)(2,1)S(1)}, bf16[512,512]{1,0:T(8,128)(2,1)S(1)}, u32[]{:S(2)}, u32[]{:S(2)}) collective-permute-start(bf16[512,512]{1,0:T(8,128)(2,1)S(1)} %constant_dynamic-update-slice_fusion.refs_0_), channel_id=1, source_target_pairs={{2,0},{4,2},{6,4},{0,6},{3,1},{5,3},{7,5},{1,7},{10,8},{12,10},{14... | collective-permute-start | bytes 1572872 | tf_op jit(solution)/shard_map/ppermute | solution.py:286
  20.5 1.2 %collective-permute-start.10 = (bf16[256,512]{1,0:T(8,128)(2,1)S(1)}, bf16[256,512]{1,0:T(8,128)(2,1)S(1)}, u32[]{:S(2)}, u32[]{:S(2)}) collective-permute-start(bf16[256,512]{1,0:T(8,128)(2,1)S(1)} %slice.9), channel_id=1, source_target_pairs={{192,0},{0,64},{64,128},{128,192},{193,1},{1,65},{65,129},{129,193... | collective-permute-start | bytes 786440 | tf_op jit(solution)/shard_map/ppermute | solution.py:289
  21.7 2.3 %collective-permute-start.8 = (bf16[256,512]{1,0:T(8,128)(2,1)S(1)}, bf16[256,512]{1,0:T(8,128)(2,1)S(1)}, u32[]{:S(2)}, u32[]{:S(2)}) collective-permute-start(bf16[256,512]{1,0:T(8,128)(2,1)S(1)} %slice.8), channel_id=1, source_target_pairs={{64,0},{128,64},{192,128},{0,192},{65,1},{129,65},{193,129},{1,193... | collective-permute-start | bytes 786440 | tf_op jit(solution)/shard_map/ppermute | solution.py:288
  24.1 1.8 %collective-permute-done.6.refs_2_ = bf16[512,512]{1,0:T(8,128)(2,1)S(1)} collective-permute-done((bf16[512,512]{1,0:T(8,128)(2,1)S(1)}, bf16[512,512]{1,0:T(8,128)(2,1)S(1)}, u32[]{:S(2)}, u32[]{:S(2)}) %collective-permute-start.6) | collective-permute-done | bytes 524320 | tf_op jit(solution)/shard_map/ppermute | solution.py:286
  25.8 11.1 %collective-permute-start.14 = (bf16[512,512]{1,0:T(8,128)(2,1)S(1)}, bf16[512,512]{1,0:T(8,128)(2,1)S(1)}, u32[]{:S(2)}, u32[]{:S(2)}) collective-permute-start(bf16[512,512]{1,0:T(8,128)(2,1)S(1)} %constant_dynamic-update-slice_fusion.refs_0_), channel_id=1, source_target_pairs={{1,0},{0,1},{3,2},{2,3},{5,4},{4,5},{7,6},{6,7},{9,8},{8,9},{11,10... | collective-permute-start | bytes 1572872 | tf_op jit(solution)/shard_map/ppermute | solution.py:292
  36.9 3.4 %collective-permute-done.12.refs_3_ = bf16[512,512]{1,0:T(8,128)(2,1)S(1)} collective-permute-done((bf16[512,512]{1,0:T(8,128)(2,1)S(1)}, bf16[512,512]{1,0:T(8,128)(2,1)S(1)}, u32[]{:S(2)}, u32[]{:S(2)}) %collective-permute-start.12) | collective-permute-done | bytes 524320 | tf_op jit(solution)/shard_map/ppermute | solution.py:286
  40.3 2.1 %collective-permute-start.13 = (bf16[512,512]{1,0:T(8,128)(2,1)S(1)}, bf16[512,512]{1,0:T(8,128)(2,1)S(1)}, u32[]{:S(2)}, u32[]{:S(2)}) collective-permute-start(bf16[512,512]{1,0:T(8,128)(2,1)S(1)} %collective-permute-done.12.refs_3_), channel_id=1, source_target_pairs={{1,0},{0,1},{3,2},{2,3},{5,4},{4,5},{7,6},{6,7},{9,8},{8,9},{11,10... | collective-permute-start | bytes 1572872 | tf_op jit(solution)/shard_map/ppermute | solution.py:292
  42.9 1.7 %project_near.1 = (f32[512,512]{1,0:T(8,128)S(1)}, f32[512,512]{1,0:T(8,128)S(1)}, bf16[4,512,512]{2,1,0:T(8,128)(2,1)S(1)}) custom-call(bf16[512,512]{1,0:T(8,128)(2,1)S(1)} %constant_dynamic-update-slice_fusion.refs_0_, bf16[512,512]{1,0:T(8,128)(2,1)S(1)} %collective-permute-done.4.refs_1_, bf16[512,512]{1,0:T(8,128)(2,1)S(1)} %collective-permute-done.6.refs_2_, ...), custom_call_target="tpu_custom_call" | custom-call | flops 1073741824 | bytes 7340032 | tf_op jit(solution)/shard_map/project_near/pallas_call | solution.py:220
  44.7 0.7 %collective-permute-done.11.refs_1_ = bf16[512,512]{1,0:T(8,128)(2,1)S(1)} collective-permute-done((bf16[512,512]{1,0:T(8,128)(2,1)S(1)}, bf16[512,512]{1,0:T(8,128)(2,1)S(1)}, u32[]{:S(2)}, u32[]{:S(2)}) %collective-permute-start.11) | collective-permute-done | bytes 524320 | tf_op jit(solution)/shard_map/ppermute | solution.py:292
  46.0 4.1 %collective-permute-start.15 = (bf16[128,512]{1,0:T(8,128)(2,1)S(1)}, bf16[128,512]{1,0:T(8,128)(2,1)S(1)}, u32[]{:S(2)}, u32[]{:S(2)}) collective-permute-start(bf16[128,512]{1,0:T(8,128)(2,1)S(1)} %get-tuple-element.51), channel_id=1, source_target_pairs={{56,0},{0,8},{8,16},{16,24},{24,32},{32,40},{40,48},{48,56},{57,1}... | collective-permute-start | bytes 393224 | tf_op jit(solution)/shard_map/ppermute | solution.py:297
  50.8 2.3 %collective-permute-start.21 = (bf16[128,512]{1,0:T(8,128)(2,1)S(1)}, bf16[128,512]{1,0:T(8,128)(2,1)S(1)}, u32[]{:S(2)}, u32[]{:S(2)}) collective-permute-start(bf16[128,512]{1,0:T(8,128)(2,1)S(1)} %get-tuple-element.55), channel_id=1, source_target_pairs={{32,0},{40,8},{48,16},{56,24},{0,32},{8,40},{16,48},{24,56},{33,1}... | collective-permute-start | bytes 393224 | tf_op jit(solution)/shard_map/ppermute | solution.py:300
  53.3 3.8 %collective-permute-start.16 = (bf16[128,512]{1,0:T(8,128)(2,1)S(1)}, bf16[128,512]{1,0:T(8,128)(2,1)S(1)}, u32[]{:S(2)}, u32[]{:S(2)}) collective-permute-start(bf16[128,512]{1,0:T(8,128)(2,1)S(1)} %add_convert_fusion.4), channel_id=1, source_target_pairs={{56,0},{0,8},{8,16},{16,24},{24,32},{32,40},{40,48},{48,56},{57,1}... | collective-permute-start | bytes 393224 | tf_op jit(solution)/shard_map/ppermute | solution.py:297
  57.2 7.2 %collective-permute-done.16 = bf16[128,512]{1,0:T(8,128)(2,1)S(1)} collective-permute-done((bf16[128,512]{1,0:T(8,128)(2,1)S(1)}, bf16[128,512]{1,0:T(8,128)(2,1)S(1)}, u32[]{:S(2)}, u32[]{:S(2)}) %collective-permute-start.16) | collective-permute-done | bytes 131104 | tf_op jit(solution)/shard_map/ppermute | solution.py:297
  64.4 2.8 %collective-permute-start.17 = (bf16[128,512]{1,0:T(8,128)(2,1)S(1)}, bf16[128,512]{1,0:T(8,128)(2,1)S(1)}, u32[]{:S(2)}, u32[]{:S(2)}) collective-permute-start(bf16[128,512]{1,0:T(8,128)(2,1)S(1)} %add_convert_fusion.3), channel_id=1, source_target_pairs={{56,0},{0,8},{8,16},{16,24},{24,32},{32,40},{40,48},{48,56},{57,1}... | collective-permute-start | bytes 393224 | tf_op jit(solution)/shard_map/ppermute | solution.py:299
  67.3 0.8 %copy.15 = bf16[512,512]{1,0:T(8,128)(2,1)} copy(bf16[512,512]{1,0:T(8,128)(2,1)S(1)} %get-tuple-element.58) | data formatting | bytes 1048576
  68.1 1.9 %collective-permute-done.17 = bf16[128,512]{1,0:T(8,128)(2,1)S(1)} collective-permute-done((bf16[128,512]{1,0:T(8,128)(2,1)S(1)}, bf16[128,512]{1,0:T(8,128)(2,1)S(1)}, u32[]{:S(2)}, u32[]{:S(2)}) %collective-permute-start.17) | collective-permute-done | bytes 131104 | tf_op jit(solution)/shard_map/ppermute | solution.py:299
  70.0 3.5 %collective-permute-done.20 = bf16[128,512]{1,0:T(8,128)(2,1)S(1)} collective-permute-done((bf16[128,512]{1,0:T(8,128)(2,1)S(1)}, bf16[128,512]{1,0:T(8,128)(2,1)S(1)}, u32[]{:S(2)}, u32[]{:S(2)}) %collective-permute-start.20) | collective-permute-done | bytes 131104 | tf_op jit(solution)/shard_map/ppermute | solution.py:299
  (39 shorter events, 5.8 us)
Async XLA Ops:
  0.6 1.0 %copy-start = (bf16[128,2048]{1,0:T(8,128)(2,1)S(1)}, bf16[128,2048]{1,0:T(8,128)(2,1)}, u32[]{:S(2)}) copy-start(bf16[128,2048]{1,0:T(8,128)(2,1)} %hidden.1) | copy-start | bytes 1572868
  1.7 8.5 %collective-permute-start = (bf16[128,512]{1,0:T(8,128)(2,1)S(1)}, bf16[128,512]{1,0:T(8,128)(2,1)S(1)}, u32[]{:S(2)}, u32[]{:S(2)}) collective-permute-start(bf16[128,512]{1,0:T(8,128)(2,1)S(1)} %get-tuple-element.33), channel_id=1, source_target_pairs={{0,0},{1,32},{8,8},{9,40},{16,16},{17,48},{24,24},{25,56},{32,1},{... | collective-permute-start | bytes 393224 | tf_op jit(solution)/shard_map/ppermute | solution.py:280
  2.4 11.0 %collective-permute-start.1 = (bf16[128,512]{1,0:T(8,128)(2,1)S(1)}, bf16[128,512]{1,0:T(8,128)(2,1)S(1)}, u32[]{:S(2)}, u32[]{:S(2)}) collective-permute-start(bf16[128,512]{1,0:T(8,128)(2,1)S(1)} %get-tuple-element.34), channel_id=1, source_target_pairs={{0,8},{1,40},{8,16},{9,48},{16,24},{17,56},{24,0},{25,32},{32,9},{... | collective-permute-start | bytes 393224 | tf_op jit(solution)/shard_map/ppermute | solution.py:280
  3.4 11.5 %collective-permute-start.2 = (bf16[128,512]{1,0:T(8,128)(2,1)S(1)}, bf16[128,512]{1,0:T(8,128)(2,1)S(1)}, u32[]{:S(2)}, u32[]{:S(2)}) collective-permute-start(bf16[128,512]{1,0:T(8,128)(2,1)S(1)} %get-tuple-element.35), channel_id=1, source_target_pairs={{0,16},{1,48},{8,24},{9,56},{16,0},{17,32},{24,8},{25,40},{32,17},... | collective-permute-start | bytes 393224 | tf_op jit(solution)/shard_map/ppermute | solution.py:280
  4.0 10.9 %collective-permute-start.3 = (bf16[128,512]{1,0:T(8,128)(2,1)S(1)}, bf16[128,512]{1,0:T(8,128)(2,1)S(1)}, u32[]{:S(2)}, u32[]{:S(2)}) collective-permute-start(bf16[128,512]{1,0:T(8,128)(2,1)S(1)} %get-tuple-element.36), channel_id=1, source_target_pairs={{0,24},{1,56},{8,0},{9,32},{16,8},{17,40},{24,16},{25,48},{32,25},... | collective-permute-start | bytes 393224 | tf_op jit(solution)/shard_map/ppermute | solution.py:280
  8.6 11.8 %collective-permute-start.9 = (bf16[512,512]{1,0:T(8,128)(2,1)S(1)}, bf16[512,512]{1,0:T(8,128)(2,1)S(1)}, u32[]{:S(2)}, u32[]{:S(2)}) collective-permute-start(bf16[512,512]{1,0:T(8,128)(2,1)S(1)} %get-tuple-element.37.refs_5_), channel_id=1, source_target_pairs={{192,0},{0,64},{64,128},{128,192},{193,1},{1,65},{65,129},{129,193... | collective-permute-start | bytes 1572872 | tf_op jit(solution)/shard_map/ppermute | solution.py:287
  10.2 11.5 %collective-permute-start.7 = (bf16[512,512]{1,0:T(8,128)(2,1)S(1)}, bf16[512,512]{1,0:T(8,128)(2,1)S(1)}, u32[]{:S(2)}, u32[]{:S(2)}) collective-permute-start(bf16[512,512]{1,0:T(8,128)(2,1)S(1)} %get-tuple-element.37.refs_5_), channel_id=1, source_target_pairs={{64,0},{128,64},{192,128},{0,192},{65,1},{129,65},{193,129},{1,193... | collective-permute-start | bytes 1572872 | tf_op jit(solution)/shard_map/ppermute | solution.py:287
  15.0 10.9 %collective-permute-start.6 = (bf16[512,512]{1,0:T(8,128)(2,1)S(1)}, bf16[512,512]{1,0:T(8,128)(2,1)S(1)}, u32[]{:S(2)}, u32[]{:S(2)}) collective-permute-start(bf16[512,512]{1,0:T(8,128)(2,1)S(1)} %constant_dynamic-update-slice_fusion.refs_0_), channel_id=1, source_target_pairs={{4,0},{6,2},{0,4},{2,6},{5,1},{7,3},{1,5},{3,7},{12,8},{14,10},{8,... | collective-permute-start | bytes 1572872 | tf_op jit(solution)/shard_map/ppermute | solution.py:286
  16.9 23.4 %collective-permute-start.12 = (bf16[512,512]{1,0:T(8,128)(2,1)S(1)}, bf16[512,512]{1,0:T(8,128)(2,1)S(1)}, u32[]{:S(2)}, u32[]{:S(2)}) collective-permute-start(bf16[512,512]{1,0:T(8,128)(2,1)S(1)} %constant_dynamic-update-slice_fusion.refs_0_), channel_id=1, source_target_pairs={{6,0},{0,2},{2,4},{4,6},{7,1},{1,3},{3,5},{5,7},{14,8},{8,10},{10,... | collective-permute-start | bytes 1572872 | tf_op jit(solution)/shard_map/ppermute | solution.py:286
  17.6 24.8 %collective-permute-start.4 = (bf16[512,512]{1,0:T(8,128)(2,1)S(1)}, bf16[512,512]{1,0:T(8,128)(2,1)S(1)}, u32[]{:S(2)}, u32[]{:S(2)}) collective-permute-start(bf16[512,512]{1,0:T(8,128)(2,1)S(1)} %constant_dynamic-update-slice_fusion.refs_0_), channel_id=1, source_target_pairs={{2,0},{4,2},{6,4},{0,6},{3,1},{5,3},{7,5},{1,7},{10,8},{12,10},{14... | collective-permute-start | bytes 1572872 | tf_op jit(solution)/shard_map/ppermute | solution.py:286
  20.5 21.9 %collective-permute-start.10 = (bf16[256,512]{1,0:T(8,128)(2,1)S(1)}, bf16[256,512]{1,0:T(8,128)(2,1)S(1)}, u32[]{:S(2)}, u32[]{:S(2)}) collective-permute-start(bf16[256,512]{1,0:T(8,128)(2,1)S(1)} %slice.9), channel_id=1, source_target_pairs={{192,0},{0,64},{64,128},{128,192},{193,1},{1,65},{65,129},{129,193... | collective-permute-start | bytes 786440 | tf_op jit(solution)/shard_map/ppermute | solution.py:289
  21.7 20.7 %collective-permute-start.8 = (bf16[256,512]{1,0:T(8,128)(2,1)S(1)}, bf16[256,512]{1,0:T(8,128)(2,1)S(1)}, u32[]{:S(2)}, u32[]{:S(2)}) collective-permute-start(bf16[256,512]{1,0:T(8,128)(2,1)S(1)} %slice.8), channel_id=1, source_target_pairs={{64,0},{128,64},{192,128},{0,192},{65,1},{129,65},{193,129},{1,193... | collective-permute-start | bytes 786440 | tf_op jit(solution)/shard_map/ppermute | solution.py:288
  25.8 17.1 %collective-permute-start.14 = (bf16[512,512]{1,0:T(8,128)(2,1)S(1)}, bf16[512,512]{1,0:T(8,128)(2,1)S(1)}, u32[]{:S(2)}, u32[]{:S(2)}) collective-permute-start(bf16[512,512]{1,0:T(8,128)(2,1)S(1)} %constant_dynamic-update-slice_fusion.refs_0_), channel_id=1, source_target_pairs={{1,0},{0,1},{3,2},{2,3},{5,4},{4,5},{7,6},{6,7},{9,8},{8,9},{11,10... | collective-permute-start | bytes 1572872 | tf_op jit(solution)/shard_map/ppermute | solution.py:292
  40.3 4.4 %collective-permute-start.13 = (bf16[512,512]{1,0:T(8,128)(2,1)S(1)}, bf16[512,512]{1,0:T(8,128)(2,1)S(1)}, u32[]{:S(2)}, u32[]{:S(2)}) collective-permute-start(bf16[512,512]{1,0:T(8,128)(2,1)S(1)} %collective-permute-done.12.refs_3_), channel_id=1, source_target_pairs={{1,0},{0,1},{3,2},{2,3},{5,4},{4,5},{7,6},{6,7},{9,8},{8,9},{11,10... | collective-permute-start | bytes 1572872 | tf_op jit(solution)/shard_map/ppermute | solution.py:292
  42.4 2.3 %collective-permute-start.5 = (bf16[512,512]{1,0:T(8,128)(2,1)S(1)}, bf16[512,512]{1,0:T(8,128)(2,1)S(1)}, u32[]{:S(2)}, u32[]{:S(2)}) collective-permute-start(bf16[512,512]{1,0:T(8,128)(2,1)S(1)} %collective-permute-done.4.refs_1_), channel_id=1, source_target_pairs={{1,0},{0,1},{3,2},{2,3},{5,4},{4,5},{7,6},{6,7},{9,8},{8,9},{11,10... | collective-permute-start | bytes 1572872 | tf_op jit(solution)/shard_map/ppermute | solution.py:292
  42.4 3.0 %collective-permute-start.11 = (bf16[512,512]{1,0:T(8,128)(2,1)S(1)}, bf16[512,512]{1,0:T(8,128)(2,1)S(1)}, u32[]{:S(2)}, u32[]{:S(2)}) collective-permute-start(bf16[512,512]{1,0:T(8,128)(2,1)S(1)} %collective-permute-done.6.refs_2_), channel_id=1, source_target_pairs={{1,0},{0,1},{3,2},{2,3},{5,4},{4,5},{7,6},{6,7},{9,8},{8,9},{11,10... | collective-permute-start | bytes 1572872 | tf_op jit(solution)/shard_map/ppermute | solution.py:292
  46.0 7.2 %collective-permute-start.15 = (bf16[128,512]{1,0:T(8,128)(2,1)S(1)}, bf16[128,512]{1,0:T(8,128)(2,1)S(1)}, u32[]{:S(2)}, u32[]{:S(2)}) collective-permute-start(bf16[128,512]{1,0:T(8,128)(2,1)S(1)} %get-tuple-element.51), channel_id=1, source_target_pairs={{56,0},{0,8},{8,16},{16,24},{24,32},{32,40},{40,48},{48,56},{57,1}... | collective-permute-start | bytes 393224 | tf_op jit(solution)/shard_map/ppermute | solution.py:297
  50.2 6.9 %collective-permute-start.18 = (bf16[128,512]{1,0:T(8,128)(2,1)S(1)}, bf16[128,512]{1,0:T(8,128)(2,1)S(1)}, u32[]{:S(2)}, u32[]{:S(2)}) collective-permute-start(bf16[128,512]{1,0:T(8,128)(2,1)S(1)} %get-tuple-element.54), channel_id=1, source_target_pairs={{8,0},{16,8},{24,16},{32,24},{40,32},{48,40},{56,48},{0,56},{9,1},... | collective-permute-start | bytes 393224 | tf_op jit(solution)/shard_map/ppermute | solution.py:298
  50.8 17.3 %collective-permute-start.21 = (bf16[128,512]{1,0:T(8,128)(2,1)S(1)}, bf16[128,512]{1,0:T(8,128)(2,1)S(1)}, u32[]{:S(2)}, u32[]{:S(2)}) collective-permute-start(bf16[128,512]{1,0:T(8,128)(2,1)S(1)} %get-tuple-element.55), channel_id=1, source_target_pairs={{32,0},{40,8},{48,16},{56,24},{0,32},{8,40},{16,48},{24,56},{33,1}... | collective-permute-start | bytes 393224 | tf_op jit(solution)/shard_map/ppermute | solution.py:300
  53.3 11.1 %collective-permute-start.16 = (bf16[128,512]{1,0:T(8,128)(2,1)S(1)}, bf16[128,512]{1,0:T(8,128)(2,1)S(1)}, u32[]{:S(2)}, u32[]{:S(2)}) collective-permute-start(bf16[128,512]{1,0:T(8,128)(2,1)S(1)} %add_convert_fusion.4), channel_id=1, source_target_pairs={{56,0},{0,8},{8,16},{16,24},{24,32},{32,40},{40,48},{48,56},{57,1}... | collective-permute-start | bytes 393224 | tf_op jit(solution)/shard_map/ppermute | solution.py:297
  57.1 10.1 %collective-permute-start.19 = (bf16[128,512]{1,0:T(8,128)(2,1)S(1)}, bf16[128,512]{1,0:T(8,128)(2,1)S(1)}, u32[]{:S(2)}, u32[]{:S(2)}) collective-permute-start(bf16[128,512]{1,0:T(8,128)(2,1)S(1)} %add_convert_fusion.2), channel_id=1, source_target_pairs={{8,0},{16,8},{24,16},{32,24},{40,32},{48,40},{56,48},{0,56},{9,1},... | collective-permute-start | bytes 393224 | tf_op jit(solution)/shard_map/ppermute | solution.py:298
  64.4 5.6 %collective-permute-start.17 = (bf16[128,512]{1,0:T(8,128)(2,1)S(1)}, bf16[128,512]{1,0:T(8,128)(2,1)S(1)}, u32[]{:S(2)}, u32[]{:S(2)}) collective-permute-start(bf16[128,512]{1,0:T(8,128)(2,1)S(1)} %add_convert_fusion.3), channel_id=1, source_target_pairs={{56,0},{0,8},{8,16},{16,24},{24,32},{32,40},{40,48},{48,56},{57,1}... | collective-permute-start | bytes 393224 | tf_op jit(solution)/shard_map/ppermute | solution.py:299
  67.2 6.3 %collective-permute-start.20 = (bf16[128,512]{1,0:T(8,128)(2,1)S(1)}, bf16[128,512]{1,0:T(8,128)(2,1)S(1)}, u32[]{:S(2)}, u32[]{:S(2)}) collective-permute-start(bf16[128,512]{1,0:T(8,128)(2,1)S(1)} %add_convert_fusion.1), channel_id=1, source_target_pairs={{8,0},{16,8},{24,16},{32,24},{40,32},{48,40},{56,48},{0,56},{9,1},... | collective-permute-start | bytes 393224 | tf_op jit(solution)/shard_map/ppermute | solution.py:299
